TPU v7x, 128 devices: a whole 4x4x4 slice. The times are simulated.
128 devices in a mesh: row: 16 (over y_lo, z, core), col: 8 (over y_hi, x).
Axes of the slice: x: 4, y: 4 (y_hi: 2, y_lo: 2; y = y_hi * 2 + y_lo), z: 4, core: 2. Of those that a mesh axis runs over, the one named last changes fastest.
Arguments:
- atom_single: bfloat16 [24576, 128], P(('row', 'col')), may hold values from -6 to 6
- pair_repr: bfloat16 [3072, 3072, 128], P('row', 'col'), may hold values from -384 to 384
- w_pair: bfloat16 [128, 4], replicated, may hold values from -0.5 to 0.5
- w_query: bfloat16 [128, 128], replicated, may hold values from -0.5 to 0.5
- w_keyval: bfloat16 [128, 256], replicated, may hold values from -0.5 to 0.5
- w_gate: bfloat16 [128, 128], replicated, may hold values from -0.5 to 0.5
- w_out: bfloat16 [128, 128], replicated, may hold values from -1.5 to 1.5
- w_agg: bfloat16 [128, 768], replicated, may hold values from -0.5 to 0.5
- atom_to_token: int32 [24576], P(('row', 'col')), may hold values from 0 to 3071, as said below
- window_shift: int32 [768], P(('row', 'col')), may hold values from -16 to 16
- atom_mask: int32 [24576], P(('row', 'col')), may hold values 0 or 1
Outputs:
- atoms: bfloat16 [24576, 128], P(('row', 'col'))
- token_single: bfloat16 [3072, 768], P('row', 'col')
Inputs may be any that keep to these rules, and one draw needn't show every extreme that they name: `atom_to_token`: atom slots k * 192 to (k + 1) * 192 - 1 name tokens k * 24 to (k + 1) * 24 - 1 only; the list never falls and every token is named at least once.
All inputs are finite; a program needn't handle non-finite values. No bound on the sum of `atom_mask` on one device may be relied on, other than what follows from the above.
Results may differ from a plain program's by a relative error of at most 0.0069.
Values may be sent and summed in bfloat16 or wider, within the bound.
A program may use at most 128 MiB of HBM per device.

v0:
```python
import jax
import jax.numpy as jnp
from jax import lax
from jax.sharding import PartitionSpec as P

QB = 32
KW = 128


NEG = -1000000000.0


def extended(array, sides, width):
    for axis, dim in sides:
        devices, length = (lax.axis_size(axis), array.shape[dim])
        up = [(i, (i + 1) % devices) for i in range(devices - 1)]
        down = [(j, i) for i, j in up]
        last = lax.slice_in_dim(array, length - width, length, axis=dim)
        initial = lax.slice_in_dim(array, 0, width, axis=dim)
        before = lax.ppermute(last, axis, up)
        after = lax.ppermute(initial, axis, down)
        array = jnp.concatenate([before, array, after], axis=dim)
    return array


def per_device(
    atom_single,
    pair_repr,
    w_pair,
    w_query,
    w_keyval,
    w_gate,
    w_out,
    w_agg,
    atom_to_token,
    window_shift,
    atom_mask,
):
    n_col = lax.axis_size("col")
    n_dev = lax.axis_size("row") * n_col
    row_index = lax.axis_index("row")
    col_index = lax.axis_index("col")
    device = row_index * n_col + col_index
    atom_dev, width = atom_single.shape
    tok_rows, tok_cols, chan = pair_repr.shape
    tok_dev = tok_rows // n_col
    heads = w_pair.shape[1]
    head_dim = width // heads
    margin = KW // 2
    n_blocks = atom_dev // QB
    table = jnp.einsum("tuc,ch->htu", pair_repr, w_pair, preferred_element_type=jnp.float32)
    slab = lax.all_gather(table, "col", axis=2, tiled=True)
    my_rows = lax.dynamic_slice_in_dim(slab, col_index * tok_dev, tok_dev, 1)
    padded = jnp.pad(my_rows, ((0, 0), (0, 0), (tok_dev, tok_dev)))
    band = lax.dynamic_slice_in_dim(padded, device * tok_dev, 3 * tok_dev, 2)
    codes = jnp.where(atom_mask == 1, atom_to_token, -1)
    keyval = jnp.dot(atom_single, w_keyval, preferred_element_type=jnp.float32).astype(jnp.bfloat16)
    keyval_ext, codes_ext = (
        extended(keyval, ((("row", "col"), 0),), margin),
        extended(codes, ((("row", "col"), 0),), margin),
    )
    position = device * atom_dev - margin + jnp.arange(atom_dev + 2 * margin, dtype=jnp.int32)
    live_ext = (codes_ext >= 0) & (position >= 0) & (position < n_dev * atom_dev)
    queries = jnp.dot(atom_single, w_query, preferred_element_type=jnp.float32).astype(jnp.bfloat16)
    gates = jax.nn.sigmoid(jnp.dot(atom_single, w_gate, preferred_element_type=jnp.float32))
    starts = QB * jnp.arange(n_blocks, dtype=jnp.int32) + QB // 2 + window_shift

    def window_of(start):
        return (
            lax.dynamic_slice_in_dim(keyval_ext, start, KW, 0),
            lax.dynamic_slice_in_dim(codes_ext, start, KW, 0),
            lax.dynamic_slice_in_dim(live_ext, start, KW, 0),
        )

    windows, key_codes, key_live = jax.vmap(window_of)(starts)
    keys = windows[:, :, :width].reshape(n_blocks, KW, heads, head_dim)
    values = windows[:, :, width:].reshape(n_blocks, KW, heads, head_dim)
    query_blocks = queries.reshape(n_blocks, QB, heads, head_dim)
    query_local = (atom_to_token - tok_dev * device).reshape(n_blocks, QB)
    query_hot = (
        query_local[:, :, None] == jnp.arange(tok_dev, dtype=jnp.int32)[None, None, :]
    ).astype(jnp.float32)
    key_local = key_codes - tok_dev * (device - 1)
    key_hot = (
        (key_local[:, :, None] == jnp.arange(3 * tok_dev, dtype=jnp.int32)[None, None, :])
        & key_live[:, :, None]
    ).astype(jnp.float32)
    row_bias = jnp.einsum("bqa,hac->bhqc", query_hot, band, precision=lax.Precision.HIGHEST)
    bias = jnp.einsum("bhqc,bkc->bhqk", row_bias, key_hot, precision=lax.Precision.HIGHEST)
    scores = jnp.einsum(
        "bqhd,bkhd->bhqk", query_blocks, keys, preferred_element_type=jnp.float32
    ) * head_dim ** (-0.5)
    scores = jnp.where(key_live[:, None, None, :], scores + bias, NEG)
    top = jnp.max(scores, axis=-1, keepdims=True)
    weights = jnp.exp(scores - top)
    probs = (weights / jnp.sum(weights, axis=-1, keepdims=True)).astype(jnp.bfloat16)
    mixed = jnp.einsum(
        "bhqk,bkhd->bqhd", probs, values, preferred_element_type=jnp.float32
    ).reshape(atom_dev, width)
    attended = (gates * mixed).astype(jnp.bfloat16)
    atoms = (
        atom_single.astype(jnp.float32)
        + jnp.dot(attended, w_out, preferred_element_type=jnp.float32)
    ).astype(jnp.bfloat16)
    lifted = jax.nn.relu(jnp.dot(atoms, w_agg, preferred_element_type=jnp.float32)).astype(
        jnp.bfloat16
    )
    own_local = atom_to_token - tok_dev * device
    member = (own_local[None, :] == jnp.arange(tok_dev, dtype=jnp.int32)[:, None]) & (
        atom_mask[None, :] == 1
    )
    sums = jnp.dot(member.astype(jnp.bfloat16), lifted, preferred_element_type=jnp.float32)
    count = jnp.sum(member.astype(jnp.float32), axis=1)
    token_local = (sums / jnp.maximum(count, 1.0)[:, None]).astype(jnp.bfloat16)
    token_single = lax.all_to_all(token_local, "col", split_axis=1, concat_axis=0, tiled=True)
    return (atoms, token_single)


def solution(mesh):
    in_specs = (
        P(("row", "col"), None),
        P("row", "col", None),
        P(),
        P(),
        P(),
        P(),
        P(),
        P(),
        P(("row", "col")),
        P(("row", "col")),
        P(("row", "col")),
    )
    out_specs = (P(("row", "col"), None), P("row", "col"))
    return jax.shard_map(
        per_device, mesh=mesh, in_specs=in_specs, out_specs=out_specs, check_vma=False
    )
```

profile of v0, /device:TPU:1, one launch (start us, length us, event | category | flops | bytes accessed | tf_op | source)
XLA Modules:
  0.0 176.7 jit_solution(1657784320196734942)
XLA Ops:
  7.3 12.4 %fusion.36 = f32[4,192,384]{2,0,1:T(4,128)} fusion(bf16[192,384,128]{2,1,0:T(8,128)(2,1)} %param.12, bf16[128,4]{0,1:T(4,128)(2,1)} %param.13), kind=kOutput, calls=%fused_computation.59 | convolution fusion | flops 75497472 | bytes 20055040 | tf_op jit(solution)/shard_map/tuc,ch->htu/dot_general | solution.py:51
  19.8 4.0 %collective-permute-start.2 = (s32[64]{0:T(128)S(1)}, s32[64]{0:T(128)S(1)}, u32[]{:S(2)}, u32[]{:S(2)}) collective-permute-start(s32[64]{0:T(128)S(1)} %get-tuple-element.56), channel_id=1, source_target_pairs={{0,1},{1,2},{2,3},{3,4},{4,5},{5,6},{6,7},{7,8},{8,9},{9,10},{10,1... | collective-permute-start | bytes 776 | tf_op jit(solution)/shard_map/ppermute | solution.py:20
  23.8 6.4 %collective-permute-start.3 = (s32[64]{0:T(128)S(1)}, s32[64]{0:T(128)S(1)}, u32[]{:S(2)}, u32[]{:S(2)}) collective-permute-start(s32[64]{0:T(128)S(1)} %get-tuple-element.57), channel_id=1, source_target_pairs={{1,0},{2,1},{3,2},{4,3},{5,4},{6,5},{7,6},{8,7},{9,8},{10,9},{11,1... | collective-permute-start | bytes 776 | tf_op jit(solution)/shard_map/ppermute | solution.py:21
  30.3 1.9 %collective-permute-start = (bf16[64,256]{1,0:T(8,128)(2,1)S(1)}, bf16[64,256]{1,0:T(8,128)(2,1)S(1)}, u32[]{:S(2)}, u32[]{:S(2)}) collective-permute-start(bf16[64,256]{1,0:T(8,128)(2,1)S(1)} %get-tuple-element.54), channel_id=1, source_target_pairs={{0,1},{1,2},{2,3},{3,4},{4,5},{5,6},{6,7},{7,8},{8,9},{9,10},{10,1... | collective-permute-start | bytes 98312 | tf_op jit(solution)/shard_map/ppermute | solution.py:20
  32.3 7.3 %collective-permute-start.1 = (bf16[64,256]{1,0:T(8,128)(2,1)S(1)}, bf16[64,256]{1,0:T(8,128)(2,1)S(1)}, u32[]{:S(2)}, u32[]{:S(2)}) collective-permute-start(bf16[64,256]{1,0:T(8,128)(2,1)S(1)} %get-tuple-element.55), channel_id=1, source_target_pairs={{1,0},{2,1},{3,2},{4,3},{5,4},{6,5},{7,6},{8,7},{9,8},{10,9},{11,1... | collective-permute-start | bytes 98312 | tf_op jit(solution)/shard_map/ppermute | solution.py:21
  40.3 8.1 %while.5 = (s32[]{:T(128)}, s32[320]{0:T(512)S(1)}, s32[6,1]{0,1:T(1,128)S(1)}, s32[6,128]{1,0:T(8,128)S(1)}, s32[]{:T(128)}, /*index=5*/s32[]{:T(128)}) while((s32[]{:T(128)}, s32[320]{0:T(512)S(1)}, s32[6,1]{0,1:T(1,128)S(1)}, s32[6,128]{1,0:T(8,128)S(1)}, s32[]{:T(128)}, /*index=5*/s32[]{:T(128)}) %tuple.53), condition=%wide.while_cond.2, body=%wide.while_body.2.sunk | while | flops 2 | bytes 2137 | solution.py:71
  40.3 0.6 constant_dynamic-slice_fusion.9
  40.9 0.7 dynamic-slice_bitcast_fusion.5
  41.6 0.6 constant_dynamic-slice_fusion.9
  42.2 0.7 dynamic-slice_bitcast_fusion.5
  42.9 0.6 constant_dynamic-slice_fusion.9
  43.6 0.7 dynamic-slice_bitcast_fusion.5
  44.3 0.6 constant_dynamic-slice_fusion.9
  44.9 0.7 dynamic-slice_bitcast_fusion.5
  45.6 0.6 constant_dynamic-slice_fusion.9
  46.2 0.7 dynamic-slice_bitcast_fusion.5
  47.0 0.6 constant_dynamic-slice_fusion.9
  47.6 0.7 dynamic-slice_bitcast_fusion.5
  48.3 8.1 %while.4 = (s32[]{:T(128)}, pred[320]{0:T(512)(128)(4,1)S(1)}, s32[6,1]{0,1:T(1,128)S(1)}, pred[6,128]{1,0:T(8,128)(4,1)S(1)}, s32[]{:T(128)}, /*index=5*/s32[]{:T(128)}) while((s32[]{:T(128)}, pred[320]{0:T(512)(128)(4,1)S(1)}, s32[6,1]{0,1:T(1,128)S(1)}, pred[6,128]{1,0:T(8,128)(4,1)S(1)}, s32[]{:T(128)}, /*index=5*/s32[]{:T(128)}) %tuple.60), condition=%wide.while_cond.1, body=%wide.while_body.1.sunk | while | flops 2 | bytes 601 | solution.py:72
  48.3 0.6 constant_dynamic-slice_fusion.8
  48.9 0.7 dynamic-slice_bitcast_fusion.4
  49.7 0.6 constant_dynamic-slice_fusion.8
  50.3 0.7 dynamic-slice_bitcast_fusion.4
  51.0 0.6 constant_dynamic-slice_fusion.8
  51.6 0.7 dynamic-slice_bitcast_fusion.4
  52.4 0.6 constant_dynamic-slice_fusion.8
  53.0 0.7 dynamic-slice_bitcast_fusion.4
  53.7 0.6 constant_dynamic-slice_fusion.8
  54.3 0.7 dynamic-slice_bitcast_fusion.4
  55.1 0.6 constant_dynamic-slice_fusion.8
  55.7 0.7 dynamic-slice_bitcast_fusion.4
  56.5 7.7 %while.3 = (s32[]{:T(128)}, bf16[320,256]{1,0:T(8,128)(2,1)S(1)}, s32[6,2]{0,1:T(2,128)S(1)}, bf16[6,128,256]{2,1,0:T(8,128)(2,1)S(1)}, s32[]{:T(128)}) while((s32[]{:T(128)}, bf16[320,256]{1,0:T(8,128)(2,1)S(1)}, s32[6,2]{0,1:T(2,128)S(1)}, bf16[6,128,256]{2,1,0:T(8,128)(2,1)S(1)}, s32[]{:T(128)}) %tuple.47), condition=%wide.while_cond, body=%wide.while_body.sunk | while | flops 2 | bytes 131169 | solution.py:70
  56.5 0.5 slice.56
  57.1 0.7 bitcast_dynamic-update-slice_fusion.2
  57.8 0.5 slice.56
  58.3 0.7 bitcast_dynamic-update-slice_fusion.2
  59.1 0.5 slice.56
  59.6 0.7 bitcast_dynamic-update-slice_fusion.2
  60.4 0.5 slice.56
  60.9 0.7 bitcast_dynamic-update-slice_fusion.2
  61.7 0.5 slice.56
  62.2 0.7 bitcast_dynamic-update-slice_fusion.2
  63.5 0.7 bitcast_dynamic-update-slice_fusion.2
  64.8 89.4 %all-gather.2.cloned.1.call-done = f32[4,192,3072]{2,0,1:T(4,128)} async-done(((f32[4,192,384]{2,0,1:T(4,128)}), f32[4,192,3072]{2,0,1:T(4,128)}) %all-gather.2.cloned.1.call-update) | async-done | bytes 9437200 | tf_op jit(solution)/shard_map/all_gather | solution.py:52
  154.2 1.3 constant_dynamic-slice_fusion.3
  156.7 1.4 convolution_bitcast_fusion
  159.3 9.9 %all_to_all.19 = bf16[24,8,96]{2,0,1:T(8,128)(2,1)S(1)} all-to-all(bf16[24,8,96]{2,0,1:T(8,128)(2,1)S(1)} %copy.33), channel_id=1, replica_groups=mesh['row'=16,'col'=8] {'col'}, dimensions={1} | all-to-all | bytes 73728 | tf_op jit(solution)/shard_map/all_to_all | solution.py:115
  169.2 0.6 copy.65
  (77 shorter events, 5.2 us)
Async XLA Ops:
  7.2 151.6 %copy-start = (bf16[128,768]{1,0:T(8,128)(2,1)S(1)}, bf16[128,768]{1,0:T(8,128)(2,1)}, u32[]{:S(2)}) copy-start(bf16[128,768]{1,0:T(8,128)(2,1)} %param.18) | copy-start | bytes 589828
  7.2 12.6 %copy-start.4 = (s32[192]{0:T(256)S(1)}, s32[192]{0:T(256)}, u32[]{:S(2)}) copy-start(s32[192]{0:T(256)} %param.19) | copy-start | bytes 2308
  7.2 12.6 %copy-start.5 = (s32[192]{0:T(256)S(1)}, s32[192]{0:T(256)}, u32[]{:S(2)}) copy-start(s32[192]{0:T(256)} %param.21) | copy-start | bytes 2308
  7.2 22.9 %copy-start.1 = (bf16[192,128]{1,0:T(8,128)(2,1)S(1)}, bf16[192,128]{1,0:T(8,128)(2,1)}, u32[]{:S(2)}) copy-start(bf16[192,128]{1,0:T(8,128)(2,1)} %param.11) | copy-start | bytes 147460
  7.2 22.9 %copy-start.2 = (bf16[128,256]{1,0:T(8,128)(2,1)S(1)}, bf16[128,256]{1,0:T(8,128)(2,1)}, u32[]{:S(2)}) copy-start(bf16[128,256]{1,0:T(8,128)(2,1)} %param.15) | copy-start | bytes 196612
  7.2 32.4 %copy-start.8 = (s32[6]{0:T(128)S(1)}, s32[6]{0:T(128)}, u32[]{:S(2)}) copy-start(s32[6]{0:T(128)} %param.20) | copy-start | bytes 76
  7.2 32.6 %copy-start.3 = (bf16[128,128]{1,0:T(8,128)(2,1)S(1)}, bf16[128,128]{1,0:T(8,128)(2,1)}, u32[]{:S(2)}) copy-start(bf16[128,128]{1,0:T(8,128)(2,1)} %param.14) | copy-start | bytes 98308
  7.2 147.0 %all-gather.2.cloned.1.call-start = ((), (), s32[]{:S(2)}) async-start(), calls=%async_computation.1 | async-start | bytes 10616832 | tf_op jit(solution)/shard_map/all_gather | solution.py:52
  19.7 138.8 %copy-start.6 = (bf16[128,128]{1,0:T(8,128)(2,1)S(1)}, bf16[128,128]{1,0:T(8,128)(2,1)}, u32[]{:S(2)}) copy-start(bf16[128,128]{1,0:T(8,128)(2,1)} %param.17) | copy-start | bytes 98308
  19.7 138.8 %copy-start.7 = (bf16[128,128]{1,0:T(8,128)(2,1)S(1)}, bf16[128,128]{1,0:T(8,128)(2,1)}, u32[]{:S(2)}) copy-start(bf16[128,128]{1,0:T(8,128)(2,1)} %param.16) | copy-start | bytes 98308
  19.8 20.3 %collective-permute-start.2 = (s32[64]{0:T(128)S(1)}, s32[64]{0:T(128)S(1)}, u32[]{:S(2)}, u32[]{:S(2)}) collective-permute-start(s32[64]{0:T(128)S(1)} %get-tuple-element.56), channel_id=1, source_target_pairs={{0,1},{1,2},{2,3},{3,4},{4,5},{5,6},{6,7},{7,8},{8,9},{9,10},{10,1... | collective-permute-start | bytes 776 | tf_op jit(solution)/shard_map/ppermute | solution.py:20
  23.8 16.3 %collective-permute-start.3 = (s32[64]{0:T(128)S(1)}, s32[64]{0:T(128)S(1)}, u32[]{:S(2)}, u32[]{:S(2)}) collective-permute-start(s32[64]{0:T(128)S(1)} %get-tuple-element.57), channel_id=1, source_target_pairs={{1,0},{2,1},{3,2},{4,3},{5,4},{6,5},{7,6},{8,7},{9,8},{10,9},{11,1... | collective-permute-start | bytes 776 | tf_op jit(solution)/shard_map/ppermute | solution.py:21
  30.3 26.1 %collective-permute-start = (bf16[64,256]{1,0:T(8,128)(2,1)S(1)}, bf16[64,256]{1,0:T(8,128)(2,1)S(1)}, u32[]{:S(2)}, u32[]{:S(2)}) collective-permute-start(bf16[64,256]{1,0:T(8,128)(2,1)S(1)} %get-tuple-element.54), channel_id=1, source_target_pairs={{0,1},{1,2},{2,3},{3,4},{4,5},{5,6},{6,7},{7,8},{8,9},{9,10},{10,1... | collective-permute-start | bytes 98312 | tf_op jit(solution)/shard_map/ppermute | solution.py:20
  32.3 24.2 %collective-permute-start.1 = (bf16[64,256]{1,0:T(8,128)(2,1)S(1)}, bf16[64,256]{1,0:T(8,128)(2,1)S(1)}, u32[]{:S(2)}, u32[]{:S(2)}) collective-permute-start(bf16[64,256]{1,0:T(8,128)(2,1)S(1)} %get-tuple-element.55), channel_id=1, source_target_pairs={{1,0},{2,1},{3,2},{4,3},{5,4},{6,5},{7,6},{8,7},{9,8},{10,9},{11,1... | collective-permute-start | bytes 98312 | tf_op jit(solution)/shard_map/ppermute | solution.py:21
  158.8 11.0 %copy-start.9 = (bf16[192,128]{1,0:T(8,128)(2,1)}, bf16[192,128]{1,0:T(8,128)(2,1)S(1)}, u32[]{:S(2)}) copy-start(bf16[192,128]{1,0:T(8,128)(2,1)S(1)} %fusion.11) | copy-start | bytes 147460
Sparse Core Ops, SparseCore 0:
  19.9 134.2 all-gather.1
where the time goes:
time: 179 us; the launch traced here: 177 us
  waiting for transfers between devices  89.4 us (50%)
  local copies, waits for them, and re-layouts  27 us (15%)
  starting transfers between devices  19.5 us (11%)
  matrix products  15.7 us (9%)
  between operations  14.4 us (8%)
  blocking collectives  9.89 us (6%)
    all_gather x1, waiting for transfers between devices, per_device(): slab = lax.all_gather(table, 'col', axis=2, tiled=True)  89.4 us
    gather x54, local copies, waits for them, and re-layouts  23.6 us
    ppermute x2, starting transfers between devices, extended(): after = lax.ppermute(initial, axis, down)  13.6 us
    dot_general x1, matrix products, per_device(): jnp.einsum('tuc,ch->htu', pair_repr, w_pair, preferred_element_type=jnp.f...  12.4 us
    all_to_all x1, blocking collectives, per_device(): lax.all_to_all(token_local, 'col', split_axis=1, concat_axis=0, tiled=True)  9.89 us
    ppermute x2, starting transfers between devices, extended(): before = lax.ppermute(last, axis, up)  5.9 us
  transfers between devices with their start and end apart: 5, of which 1 were waited for; matrix products, arithmetic and copies ran while one was open for 14% of the time, Pallas kernels for 0%

commit v1 on v0

v1 whole, which is shorter than its diff:
```python
import functools
import math

import jax
import jax.numpy as jnp
from jax import lax
from jax.experimental import pallas as pl
from jax.experimental.pallas import tpu as pltpu
from jax.sharding import PartitionSpec as P

MESH = pl.DeviceIdType.MESH

QB = 32
KW = 128
WIDE = 80
SIDE = 48
OUTSIDE = -1.0e30
DEAD = -1.0e9
F32 = jnp.float32
BF16 = jnp.bfloat16


def dot(a, b):
    return jnp.dot(a, b, preferred_element_type=F32)


def dot_nt(a, b):
    return lax.dot_general(a, b, (((1,), (1,)), ((), ())), preferred_element_type=F32)


def kernel(
    n_row,
    n_col,
    x_in,
    pair_in,
    wp_in,
    wq_in,
    wkv_in,
    wg_in,
    wo_in,
    wa_in,
    tok_in,
    shift_in,
    mask_in,
    atoms_out,
    tok_recv,
    xs,
    strips,
    corner_x,
    wp,
    wq,
    wkv,
    wg,
    wo,
    wa,
    wa_pad,
    tok,
    mask,
    shift,
    tsend,
    csend,
    table,
    corner,
    messages,
    left_codes,
    right_codes,
    lhs,
    tok_send,
    in_sem,
    strip_sem,
    halo_send,
    halo_recv,
    table_send,
    table_recv,
    corner_send,
    corner_recv,
    tok_ssem,
    tok_rsem,
    ready,
    hello,
    go,
    corner_ready,
):
    row = lax.axis_index("row")
    col = lax.axis_index("col")
    me = row * n_col + col
    n_dev = n_row * n_col
    atoms = x_in.shape[0]
    width = x_in.shape[1]
    tok_rows, tok_cols, chan = pair_in.shape
    tok_dev = tok_rows // n_col
    half_t = tok_dev // 2
    heads = wp_in.shape[0]
    head_dim = width // heads
    margin = KW // 2
    per_col = tok_cols // tok_rows
    hold_col = row // per_col
    odd = row % per_col == per_col - 1
    even = row % per_col == 0
    is_holder = col == hold_col
    base = (row % per_col) * tok_rows

    def strip_start(j):
        want = base + tok_dev * (j - 1)
        want = jnp.maximum(want, 0)
        return jnp.minimum((want // 16) * 16, tok_cols - WIDE)

    has_left = me > 0
    has_right = me < n_dev - 1
    last = n_col - 1
    barrier = pltpu.get_barrier_semaphore()

    def edge(a, b):
        low = even & (b == hold_col - 1) & (a == 0)
        high = odd & (b == last) & (a == hold_col + 1)
        return (a != b) & ((a == hold_col) | (a == b - 1) | low | high)

    expected = jnp.where((col == last) & has_right, 1, 0)
    for other in range(n_col):
        expected = expected + jnp.where(edge(other, col), 1, 0)

        @pl.when(edge(col, other))
        def _():
            pl.semaphore_signal(barrier, inc=1, device_id=(row, other), device_id_type=MESH)

    @pl.when((col == 0) & has_left)
    def _():
        pl.semaphore_signal(barrier, inc=1, device_id=(row - 1, last), device_id_type=MESH)

    def local(i, src, dst):
        return pltpu.make_async_copy(src, dst, in_sem.at[i])

    wp_copy = local(0, wp_in, wp)
    x_copy = local(1, x_in, xs.at[pl.ds(0, atoms)])
    tok_copy = local(2, tok_in, tok)
    mask_copy = local(3, mask_in, mask)
    shift_copy = local(4, shift_in, shift)
    wkv_copy = local(5, wkv_in, wkv)
    wq_copy = local(6, wq_in, wq)
    wg_copy = local(7, wg_in, wg)
    wo_copy = local(8, wo_in, wo)
    wa_copy = local(9, wa_in, wa)
    wp_copy.start()

    def strip_copy(j):
        start = pl.multiple_of(strip_start(j), 16)
        return pltpu.make_async_copy(
            pair_in.at[pl.ds(tok_dev * j, tok_dev), pl.ds(start, WIDE)],
            strips.at[j],
            strip_sem.at[j],
        )

    x_copy.start()
    tok_copy.start()
    mask_copy.start()

    @pl.when(is_holder)
    def _():
        for j in range(n_col):
            strip_copy(j).start()

    shift_copy.start()
    wkv_copy.start()
    wq_copy.start()
    wg_copy.start()
    wo_copy.start()
    wa_copy.start()

    corner_to = jnp.where(even, 0, n_col - 1)
    give_even = even & (col == hold_col - 1)
    give_odd = odd & (col == hold_col + 1)
    gives_corner = give_even | give_odd
    takes_corner = (even & (row > 0) & (col == 0)) | (
        odd & (row < n_row - 1) & (col == n_col - 1)
    )
    corner_here = gives_corner & takes_corner
    corner_away = gives_corner & jnp.logical_not(takes_corner)
    corner_comes = takes_corner & jnp.logical_not(gives_corner)
    corner_col = pl.multiple_of(jnp.where(even, tok_cols - SIDE, 0), 16)
    corner_row = pl.multiple_of(jnp.where(even, 0, tok_rows - tok_dev), 8)
    corner_copy = pltpu.make_async_copy(
        pair_in.at[pl.ds(corner_row, tok_dev), pl.ds(corner_col, SIDE)], corner_x, in_sem.at[10]
    )

    @pl.when(gives_corner)
    def _():
        corner_copy.start()

    @pl.when(jnp.logical_not(corner_comes))
    def _():
        corner[...] = jnp.zeros_like(corner)

    left_id = (jnp.where(col > 0, row, row - 1), (col + n_col - 1) % n_col)
    right_id = (jnp.where(col < last, row, row + 1), (col + 1) % n_col)

    @pl.when(expected > 0)
    def _():
        pl.semaphore_wait(barrier, expected)

    @pl.when(jnp.logical_not(is_holder))
    def _():
        pl.semaphore_signal(
            ready.at[col], inc=1, device_id=(row, hold_col), device_id_type=MESH
        )

    @pl.when(col > 0)
    def _():
        pl.semaphore_signal(hello.at[0], inc=1, device_id=left_id, device_id_type=MESH)

    @pl.when((col == last) & has_right)
    def _():
        pl.semaphore_signal(hello.at[1], inc=1, device_id=right_id, device_id_type=MESH)

    corner_asks = corner_comes & odd

    @pl.when(corner_asks)
    def _():
        pl.semaphore_signal(
            corner_ready, inc=1, device_id=(row, hold_col + 1), device_id_type=MESH
        )

    wp_copy.wait()
    w_one = wp[...].astype(F32)
    w_rows = jnp.concatenate([w_one, w_one], axis=0)
    first_half = lax.broadcasted_iota(jnp.int32, w_rows.shape, 0) < heads
    w_both = jnp.concatenate(
        [jnp.where(first_half, w_rows, 0.0), jnp.where(first_half, 0.0, w_rows)], axis=1
    ).astype(BF16)

    def project(block):
        count = half_t * block.shape[1]
        low = block[:half_t].reshape(count, chan)
        high = block[half_t:].reshape(count, chan)
        return dot_nt(w_both, jnp.concatenate([low, high], axis=1))

    def corner_send_copy():
        return pltpu.make_async_remote_copy(
            src_ref=csend,
            dst_ref=corner,
            send_sem=corner_send,
            recv_sem=corner_recv,
            device_id=(row, corner_to),
            device_id_type=MESH,
        )

    def table_send_copy(j):
        return pltpu.make_async_remote_copy(
            src_ref=tsend.at[j],
            dst_ref=table,
            send_sem=table_send.at[j],
            recv_sem=table_recv,
            device_id=(row, j),
            device_id_type=MESH,
        )

    x_copy.wait()
    tok_copy.wait()
    mask_copy.wait()
    tokens = jnp.concatenate(
        [tok[...].reshape(1, atoms), jnp.full((1, 2 * width - atoms), -1, jnp.int32)], axis=1
    )
    masks = jnp.concatenate(
        [mask[...].reshape(1, atoms), jnp.zeros((1, 2 * width - atoms), jnp.int32)], axis=1
    )
    codes = jnp.where(masks == 1, tokens, -1)
    codes0, codes1 = codes[:, :width], codes[:, width:]
    messages[0] = jnp.broadcast_to(pltpu.roll(codes0, margin, 1), (8, width))
    messages[1] = jnp.broadcast_to(pltpu.roll(codes1, margin, 1), (8, width))

    def halo(i, src, dst, device):
        return pltpu.make_async_remote_copy(
            src_ref=src,
            dst_ref=dst,
            send_sem=halo_send.at[i],
            recv_sem=halo_recv.at[i],
            device_id=device,
            device_id_type=MESH,
        )

    to_left = (
        halo(0, xs.at[pl.ds(0, margin)], xs.at[pl.ds(atoms + margin, margin)], left_id),
        halo(1, messages.at[0], right_codes, left_id),
    )
    to_right = (
        halo(2, xs.at[pl.ds(atoms - margin, margin)], xs.at[pl.ds(atoms, margin)], right_id),
        halo(3, messages.at[1], left_codes, right_id),
    )

    @pl.when(jnp.logical_not(has_left))
    def _():
        xs[pl.ds(atoms, margin)] = jnp.zeros((margin, width), BF16)
        left_codes[...] = jnp.full(left_codes.shape, -1, jnp.int32)

    @pl.when(jnp.logical_not(has_right))
    def _():
        xs[pl.ds(atoms + margin, margin)] = jnp.zeros((margin, width), BF16)
        right_codes[...] = jnp.full(right_codes.shape, -1, jnp.int32)

    @pl.when(col > 0)
    def _():
        for copy in to_left:
            copy.start()

    @pl.when((col == last) & has_right)
    def _():
        for copy in to_right:
            copy.start()

    x_own = xs[pl.ds(0, atoms)]
    wq_copy.wait()
    queries = dot(x_own, wq[...])
    lanes = lax.broadcasted_iota(jnp.int32, (atoms, width), 1)
    local_tok = tokens - tok_dev * me
    upper = local_tok >= half_t
    place = jnp.where(upper, (local_tok - half_t) * 8 + heads, local_tok * 8)
    place = jnp.transpose(jnp.broadcast_to(place, (width, 2 * width)))[:atoms]
    first = atoms - margin
    for h in range(heads):
        q_h = jnp.where(lanes // head_dim == h, queries, 0.0).astype(BF16)
        hot_h = (lanes - h == place).astype(F32).astype(BF16)
        lhs[pl.ds(h * first, first), pl.ds(0, width)] = q_h[:first]
        lhs[pl.ds(h * first, first), pl.ds(width, width)] = hot_h[:first]
        lhs[pl.ds(heads * first + h * margin, margin), pl.ds(0, width)] = q_h[first:]
        lhs[pl.ds(heads * first + h * margin, margin), pl.ds(width, width)] = hot_h[first:]
    wg_copy.wait()
    gates = jax.nn.sigmoid(dot(x_own, wg[...]))
    wa_copy.wait()
    share = wa.shape[1] // n_col
    for c in range(n_col):
        part = jnp.concatenate(
            [wa[:, c * share : (c + 1) * share], jnp.zeros((width, width - share), BF16)], axis=1
        )
        wa_pad[:, c * width : (c + 1) * width] = part
    member = lax.broadcasted_iota(jnp.int32, (32, atoms), 0) == (codes - tok_dev * me)[:, :atoms]
    member = member.astype(F32)
    count = jnp.sum(member, axis=1, keepdims=True)
    inverse = 1.0 / jnp.maximum(count, 1.0)
    member = member.astype(BF16)

    group = n_col // 2

    @pl.when(is_holder)
    def _():
        for start in range(0, n_col, group):
            for j in range(start, start + group):
                strip_copy(j).wait()
            for j in range(start, start + group):
                tsend[j] = project(strips[j])
            for j in range(start, start + group):

                @pl.when(col != j)
                def _():
                    pl.semaphore_wait(ready.at[j], 1)
                    table_send_copy(j).start()

        for step in range(1, n_col):
            pl.semaphore_signal(
                go, inc=1, device_id=(row, (col + step) % n_col), device_id_type=MESH
            )
        table[...] = tsend[col]

    @pl.when(col < last)
    def _():
        pl.semaphore_wait(hello.at[0], 1)
        for copy in to_right:
            copy.start()

    @pl.when((col == 0) & has_left)
    def _():
        pl.semaphore_wait(hello.at[1], 1)
        for copy in to_left:
            copy.start()

    @pl.when(gives_corner)
    def _():
        corner_copy.wait()
        csend[...] = project(corner_x[...])

    @pl.when(corner_away & odd)
    def _():
        pl.semaphore_wait(corner_ready, 1)

    @pl.when(corner_away)
    def _():
        corner_send_copy().start()

    @pl.when(corner_here)
    def _():
        corner[...] = csend[...]

    @pl.when(has_left)
    def _():
        for copy in to_right:
            copy.wait_recv()

    @pl.when(has_right)
    def _():
        for copy in to_left:
            copy.wait_recv()

    wkv_copy.wait()
    keyval = dot(xs[...], wkv[...])
    keys_t = jnp.transpose(keyval[:, :width])
    keys_t = keys_t.astype(BF16)
    values = keyval[:, width:].astype(BF16)
    ones = jnp.ones((atoms + margin, width), BF16)
    v_a = jnp.concatenate([values[: atoms + margin], ones], axis=1)
    v_b = jnp.concatenate(
        [jnp.concatenate([values[:atoms], values[atoms + margin :]], axis=0), ones], axis=1
    )
    k_a = keys_t[:, : atoms + margin]
    k_b = jnp.concatenate([keys_t[:, :atoms], keys_t[:, atoms + margin :]], axis=1)
    side = lax.broadcasted_iota(jnp.int32, (1, width), 1)
    codes_a = jnp.where(side < margin, codes1, left_codes[0:1])
    codes_b = jnp.where(side < margin, codes1, right_codes[0:1])
    shift_copy.wait()
    lane2 = lax.broadcasted_iota(jnp.int32, (1, 2 * width), 1)
    at_a = jnp.where(lane2 < atoms, lane2, lane2 - 2 * width)
    full_a = jnp.concatenate([codes0, codes_a], axis=1)
    full_b = jnp.concatenate([codes0, codes_b], axis=1)
    caps = []
    for b in range(atoms // QB):
        start = QB * b - KW // 2 + QB // 2 + shift[b]
        at = at_a if b * QB < first else lane2
        code = full_a if b * QB < first else full_b
        inside = (at >= start) & (at < start + KW)
        cap = jnp.where(inside, jnp.where(code >= 0, 3.0e38, DEAD), OUTSIDE)
        caps.append(cap)

    @pl.when(jnp.logical_not(is_holder))
    def _():
        table_send_copy(0).wait_recv()

    @pl.when(corner_comes)
    def _():
        corner_send_copy().wait_recv()

    main = table[...]
    edge = corner[...]
    rows = [
        jnp.concatenate(
            [main[:, WIDE * t : WIDE * (t + 1)], edge[:, SIDE * t : SIDE * (t + 1)]], axis=1
        )
        for t in range(half_t)
    ]
    stacked = jnp.concatenate(rows, axis=0) * math.sqrt(head_dim)
    first_token = hold_col * tok_cols + strip_start(col)

    def spread(code):
        index = jnp.broadcast_to((code - first_token) & (width - 1), stacked.shape)
        return jnp.take_along_axis(stacked, index, axis=1, mode="promise_in_bounds")

    g_0, g_a, g_b = spread(codes0), spread(codes_a), spread(codes_b)
    pad_rows = jnp.zeros((width - stacked.shape[0], 2 * width), F32)

    def pieces(second):
        whole = jnp.concatenate([jnp.concatenate([g_0, second], axis=1), pad_rows], axis=0)
        high = whole.astype(BF16)
        rest = whole - high.astype(F32)
        mid = rest.astype(BF16)
        low = (rest - mid.astype(F32)).astype(BF16)
        return [high, mid, low]

    log_scale = math.log2(math.e) / math.sqrt(head_dim)

    def attend(first_row, n_rows, keys, second, vals, cap_list):
        both = lhs[pl.ds(first_row, heads * n_rows), :]
        hot = both[:, width:]
        left = jnp.concatenate([both, hot, hot], axis=1)
        right = jnp.concatenate([keys] + pieces(second), axis=0)
        scores = dot(left, right)
        parts = []
        per = n_rows // QB
        for i in range(heads * per):
            part = jnp.minimum(scores[i * QB : (i + 1) * QB], cap_list[i % per])
            top = jnp.max(part, axis=1, keepdims=True)
            parts.append(jnp.exp2((part - top) * log_scale).astype(BF16))
        weights = jnp.concatenate(parts, axis=0)
        mixed = dot(weights, vals)
        value, total = mixed[:n_rows, :width], mixed[:n_rows, width:]
        group = lax.broadcasted_iota(jnp.int32, (n_rows, width), 1) // head_dim
        for h in range(1, heads):
            value = jnp.where(group == h, mixed[h * n_rows : (h + 1) * n_rows, :width], value)
            total = jnp.where(group == h, mixed[h * n_rows : (h + 1) * n_rows, width:], total)
        return value / total

    n_a = first // QB
    out_a = attend(0, first, k_a, g_a, v_a, caps[:n_a])
    out_b = attend(heads * first, margin, k_b, g_b, v_b, caps[n_a:])
    attended = (gates * jnp.concatenate([out_a, out_b], axis=0)).astype(BF16)
    wo_copy.wait()
    new_atoms = (x_own.astype(F32) + dot(attended, wo[...])).astype(BF16)
    atoms_out[...] = new_atoms
    lifted = jnp.maximum(dot(new_atoms, wa_pad[...]), 0.0).astype(BF16)
    means = (dot(member, lifted) * inverse)[:tok_dev].astype(BF16)
    for c in range(n_col):
        tok_send[c] = means[:, c * width : (c + 1) * width]

    def tok_copy_to(step):
        other = (col + step) % n_col
        return pltpu.make_async_remote_copy(
            src_ref=tok_send.at[other],
            dst_ref=tok_recv.at[col],
            send_sem=tok_ssem.at[other],
            recv_sem=tok_rsem.at[col],
            device_id=(row, other),
            device_id_type=MESH,
        )

    def tok_copy_from(step):
        other = (col + step) % n_col
        return pltpu.make_async_remote_copy(
            src_ref=tok_send.at[other],
            dst_ref=tok_recv.at[other],
            send_sem=tok_ssem.at[other],
            recv_sem=tok_rsem.at[other],
            device_id=(row, other),
            device_id_type=MESH,
        )

    @pl.when(jnp.logical_not(is_holder))
    def _():
        pl.semaphore_wait(go, 1)

    for step in range(1, n_col):
        tok_copy_to(step).start()
    tok_recv[col] = tok_send[col]
    for step in range(1, n_col):
        tok_copy_from(step).wait_recv()

    for step in range(1, n_col):
        tok_copy_to(step).wait_send()

    @pl.when(is_holder)
    def _():
        for j in range(n_col):

            @pl.when(col != j)
            def _():
                table_send_copy(j).wait_send()

    @pl.when(corner_away)
    def _():
        corner_send_copy().wait_send()

    @pl.when(has_left)
    def _():
        for copy in to_left:
            copy.wait_send()

    @pl.when(has_right)
    def _():
        for copy in to_right:
            copy.wait_send()


def finish(atoms_ref, gathered, atoms_out, token_out, token_v, sems):
    atoms_copy = pltpu.make_async_copy(atoms_ref, atoms_out, sems.at[0])
    atoms_copy.start()
    rows = jnp.concatenate(
        [gathered[c].astype(F32) for c in range(gathered.shape[0])], axis=0
    )
    token_v[...] = rows.astype(BF16)[:, : token_v.shape[1]]
    token_copy = pltpu.make_async_copy(token_v, token_out, sems.at[1])
    token_copy.start()
    atoms_copy.wait()
    token_copy.wait()


def per_device(n_row, n_col, *args):
    x, pair, w_pair, w_query, w_keyval, w_gate, w_out, w_agg, tok, shift, mask = args
    w_pair = w_pair.T
    atoms, width = x.shape
    tok_rows, tok_cols, chan = pair.shape
    heads = w_pair.shape[0]
    tok_dev = tok_rows // n_col
    half_t = tok_dev // 2
    ct = w_agg.shape[1]
    margin = KW // 2
    hbm = pl.BlockSpec(memory_space=pltpu.HBM)
    vmem = pl.BlockSpec(memory_space=pltpu.VMEM)
    dma = pltpu.SemaphoreType.DMA
    regular = pltpu.SemaphoreType.REGULAR
    scratch = [
        pltpu.VMEM((atoms + 2 * margin, width), BF16),
        pltpu.VMEM((n_col, tok_dev, WIDE, chan), BF16),
        pltpu.VMEM((tok_dev, SIDE, chan), BF16),
        pltpu.VMEM(w_pair.shape, BF16),
        pltpu.VMEM(w_query.shape, BF16),
        pltpu.VMEM(w_keyval.shape, BF16),
        pltpu.VMEM(w_gate.shape, BF16),
        pltpu.VMEM(w_out.shape, BF16),
        pltpu.VMEM(w_agg.shape, BF16),
        pltpu.VMEM((width, n_col * width), BF16),
        pltpu.VMEM(tok.shape, jnp.int32),
        pltpu.VMEM(mask.shape, jnp.int32),
        pltpu.SMEM(shift.shape, jnp.int32),
        pltpu.VMEM((n_col, 2 * heads, half_t * WIDE), F32),
        pltpu.VMEM((2 * heads, half_t * SIDE), F32),
        pltpu.VMEM((2 * heads, half_t * WIDE), F32),
        pltpu.VMEM((2 * heads, half_t * SIDE), F32),
        pltpu.VMEM((2, 8, width), jnp.int32),
        pltpu.VMEM((8, width), jnp.int32),
        pltpu.VMEM((8, width), jnp.int32),
        pltpu.VMEM((heads * atoms, 2 * width), BF16),
        pltpu.VMEM((n_col, tok_dev, width), BF16),
        dma((11,)),
        dma((n_col,)),
        dma((4,)),
        dma((4,)),
        dma((n_col,)),
        dma,
        dma,
        dma,
        dma((n_col,)),
        dma((n_col,)),
        regular((n_col,)),
        regular((2,)),
        regular,
        regular,
    ]
    inputs = (x, pair, w_pair, w_query, w_keyval, w_gate, w_out, w_agg, tok, shift, mask)
    inputs = [pltpu.with_memory_space_constraint(a, pltpu.HBM) for a in inputs]
    new_atoms, gathered = pl.pallas_call(
        functools.partial(kernel, n_row, n_col),
        out_shape=(
            pltpu.VMEM((atoms, width), BF16),
            pltpu.VMEM((n_col, tok_dev, width), BF16),
        ),
        in_specs=[hbm] * 11,
        out_specs=(vmem, vmem),
        scratch_shapes=scratch,
        compiler_params=pltpu.CompilerParams(
            collective_id=0, has_side_effects=True, vmem_limit_bytes=40 * 1024 * 1024
        ),
        name="atom_block",
    )(*inputs)
    return pl.pallas_call(
        finish,
        out_shape=(
            pltpu.HBM((atoms, width), BF16),
            pltpu.HBM((tok_rows, ct // n_col), BF16),
        ),
        in_specs=[vmem, vmem],
        out_specs=(hbm, hbm),
        scratch_shapes=[pltpu.VMEM((tok_rows, ct // n_col), BF16), dma((2,))],
        compiler_params=pltpu.CompilerParams(vmem_limit_bytes=8 * 1024 * 1024),
        name="write_out",
    )(new_atoms, gathered)


def solution(mesh):
    n_row, n_col = mesh.shape["row"], mesh.shape["col"]
    split = P(("row", "col"))
    in_specs = (
        P(("row", "col"), None),
        P("row", "col", None),
        P(),
        P(),
        P(),
        P(),
        P(),
        P(),
        split,
        split,
        split,
    )
    out_specs = (P(("row", "col"), None), P("row", "col"))
    return jax.shard_map(
        functools.partial(per_device, n_row, n_col),
        mesh=mesh,
        in_specs=in_specs,
        out_specs=out_specs,
        check_vma=False,
    )
```

time: 179 us -> 20.9 us (0.12); the launches traced: 177 us -> 20.8 us
  waiting for transfers between devices: 89.4 us -> 0 us
  local copies, waits for them, and re-layouts: 27 us -> 0 us
  Pallas kernels: 0 us -> 20.2 us
  starting transfers between devices: 19.5 us -> 0 us
  matrix products: 15.7 us -> 0 us
  between operations: 14.4 us -> 0.64 us
  blocking collectives: 9.89 us -> 0 us
    all_gather x1 -> x0, waiting for transfers between devices: 89.4 us -> none  [per_device(): slab = lax.all_gather(table, 'col', axis=2, tiled=True)]
    gather x54 -> x0, local copies, waits for them, and re-layouts: 23.6 us -> none
    pallas_call x0 -> x2, Pallas kernels: none -> 20.2 us  [the longest x1 19.5 us: per_device(): pl.pallas_call(functools.partial(kernel, n_row, n_col), out_shape=(pltpu....]
    ppermute x4 -> x0, starting transfers between devices: 19.5 us -> none  [the longest x2 13.6 us: extended(): after = lax.ppermute(initial, axis, down)]
    dot_general x9 -> x0, matrix products: 15.7 us -> none  [the longest x1 12.4 us: per_device(): jnp.einsum('tuc,ch->htu', pair_repr, w_pair, preferred_element_type=jnp.f...]
    all_to_all x1 -> x0, blocking collectives: 9.89 us -> none  [per_device(): lax.all_to_all(token_local, 'col', split_axis=1, concat_axis=0, tiled=True)]
  transfers between devices with their start and end apart: 5 -> 0, of which waited for: 1 -> 0; matrix products, arithmetic and copies ran while one was open for 14% -> 0% of each run, Pallas kernels for 0% -> 0%
where the time goes in v1:
time: 20.9 us; the launch traced here: 20.8 us
  Pallas kernels  20.2 us (97%)
  between operations  0.64 us (3%)
    pallas_call x1, Pallas kernels, per_device(): pl.pallas_call(functools.partial(kernel, n_row, n_col), out_shape=(pltpu....  19.5 us
    pallas_call x1, Pallas kernels, per_device(): pl.pallas_call(finish, out_shape=(pltpu.HBM((atoms, width), BF16), pltpu....  0.66 us

profile of v1, /device:TPU:1, one launch (start us, length us, event | category | flops | bytes accessed | tf_op | source)
XLA Modules:
  0.0 20.8 jit_solution(171898333210876534)
XLA Ops:
  0.6 19.5 %atom_block.1 = (bf16[192,128]{1,0:T(8,128)(2,1)S(1)}, bf16[8,24,128]{2,1,0:T(8,128)(2,1)S(1)}) custom-call(bf16[192,128]{1,0:T(8,128)(2,1)} %x_in.1, bf16[192,384,128]{2,1,0:T(8,128)(2,1)} %pair_in.1, bf16[4,128]{1,0:T(4,128)(2,1)} %bitcast.1, bf16[128,128]{1,0:T(8,128)(2,1)} %wq_in.1, bf16[128,256]{1,0:T(8,128)(2,1)} %wkv_in.1, bf16[128,128]{1,0:T(8,128)(2,1)} %wg_in.1, ...), custom_call_target="tpu_custom_call" | custom-call | tf_op jit(solution)/shard_map/atom_block/pallas_call | solution.py:624
  20.2 0.7 %write_out.1 = (bf16[192,128]{1,0:T(8,128)(2,1)}, bf16[192,96]{1,0:T(8,128)(2,1)}) custom-call(bf16[192,128]{1,0:T(8,128)(2,1)S(1)} %get-tuple-element.4.atoms_ref, bf16[8,24,128]{2,1,0:T(8,128)(2,1)S(1)} %get-tuple-element.5.gathered), custom_call_target="tpu_custom_call" | custom-call | tf_op jit(solution)/shard_map/write_out/pallas_call | solution.py:638

commit v2 on v1

v2 whole, which is shorter than its diff:
```python
import functools
import math

import jax
import jax.numpy as jnp
from jax import lax
from jax.experimental import pallas as pl
from jax.experimental.pallas import tpu as pltpu
from jax.sharding import PartitionSpec as P

MESH = pl.DeviceIdType.MESH

QB = 32
KW = 128
WIDE = 80
SIDE = 48
OUTSIDE = -(2.0**126)
DEAD = -(2.0**100)
F32 = jnp.float32
BF16 = jnp.bfloat16


def dot(a, b):
    return jnp.dot(a, b, preferred_element_type=F32)


def dot_nt(a, b):
    return lax.dot_general(a, b, (((1,), (1,)), ((), ())), preferred_element_type=F32)


def kernel(
    n_row,
    n_col,
    x_in,
    pair_in,
    wp_in,
    wq_in,
    wkv_in,
    wg_in,
    wo_in,
    wa_in,
    tok_in,
    shift_in,
    mask_in,
    atoms_out,
    tok_recv,
    xs,
    strips,
    corner_x,
    wp,
    wq,
    wkv,
    wg,
    wo,
    wa,
    tok,
    mask,
    shift,
    tsend,
    csend,
    table,
    corner,
    messages,
    codes_s,
    lhs,
    rhs,
    vals,
    tok_send,
    in_sem,
    strip_sem,
    halo_send,
    halo_recv,
    table_send,
    table_recv,
    corner_send,
    corner_recv,
    tok_ssem,
    tok_rsem,
):
    row = lax.axis_index("row")
    col = lax.axis_index("col")
    me = row * n_col + col
    n_dev = n_row * n_col
    atoms, width = x_in.shape
    tok_rows, tok_cols, chan = pair_in.shape
    tok_dev = tok_rows // n_col
    half_t = tok_dev // 2
    heads = wp_in.shape[0]
    head_dim = width // heads
    margin = KW // 2
    per_col = tok_cols // tok_rows
    hold_col = row // per_col
    odd = row % per_col == per_col - 1
    even = row % per_col == 0
    is_holder = col == hold_col
    base = (row % per_col) * tok_rows
    has_left = me > 0
    has_right = me < n_dev - 1

    def strip_start(j):
        want = jnp.maximum(base + tok_dev * (j - 1), 0)
        return jnp.minimum((want // 16) * 16, tok_cols - WIDE)

    barrier = pltpu.get_barrier_semaphore()

    for step in range(1, n_col):
        other = (col + step) % n_col
        pl.semaphore_signal(barrier, inc=1, device_id=(row, other), device_id_type=MESH)

    up_row = (col == 0) & has_left
    down_row = (col == n_col - 1) & has_right
    left_id = (jnp.where(col > 0, row, row - 1), (col + n_col - 1) % n_col)
    right_id = (jnp.where(col < n_col - 1, row, row + 1), (col + 1) % n_col)

    @pl.when(up_row)
    def _():
        pl.semaphore_signal(barrier, inc=1, device_id=left_id, device_id_type=MESH)

    @pl.when(down_row)
    def _():
        pl.semaphore_signal(barrier, inc=1, device_id=right_id, device_id_type=MESH)

    expected = n_col - 1 + up_row.astype(jnp.int32) + down_row.astype(jnp.int32)

    def local(i, src, dst):
        return pltpu.make_async_copy(src, dst, in_sem.at[i])

    tail = atoms - margin
    x_copy = local(0, x_in, xs.at[pl.ds(0, atoms)])
    tail_copy = local(1, x_in.at[pl.ds(tail, margin)], xs.at[pl.ds(2 * width, margin)])
    toks_copy = local(2, tok_in, tok)
    mask_copy = local(3, mask_in, mask)
    wp_copy = local(4, wp_in, wp)
    wq_copy = local(5, wq_in, wq)
    wg_copy = local(6, wg_in, wg)
    wkv_copy = local(7, wkv_in, wkv)
    shift_copy = local(8, shift_in, shift)
    wo_copy = local(9, wo_in, wo)
    wa_copy = local(10, wa_in, wa)

    def strip_copy(s):
        j = (col + 1 + s) % n_col
        start = pl.multiple_of(strip_start(j), 16)
        return pltpu.make_async_copy(
            pair_in.at[pl.ds(pl.multiple_of(tok_dev * j, 8), tok_dev), pl.ds(start, WIDE)],
            strips.at[s],
            strip_sem.at[s],
        )

    x_copy.start()
    toks_copy.start()
    mask_copy.start()
    wp_copy.start()

    @pl.when(is_holder)
    def _():
        for s in range(n_col):
            strip_copy(s).start()

    wq_copy.start()
    wg_copy.start()
    tail_copy.start()
    wkv_copy.start()
    shift_copy.start()
    wo_copy.start()
    wa_copy.start()

    corner_to = jnp.where(even, 0, n_col - 1)
    gives_corner = (even & (col == hold_col - 1)) | (odd & (col == hold_col + 1))
    takes_corner = (up_row & even) | (down_row & odd)
    corner_comes = takes_corner & jnp.logical_not(gives_corner)
    corner_away = gives_corner & jnp.logical_not(takes_corner)
    corner_col = pl.multiple_of(jnp.where(even, tok_cols - SIDE, 0), 16)
    corner_row = pl.multiple_of(jnp.where(even, 0, tok_rows - tok_dev), 8)
    corner_copy = pltpu.make_async_copy(
        pair_in.at[pl.ds(corner_row, tok_dev), pl.ds(corner_col, SIDE)], corner_x, in_sem.at[11]
    )

    @pl.when(gives_corner)
    def _():
        corner_copy.start()

    @pl.when(jnp.logical_not(corner_comes))
    def _():
        corner[...] = jnp.zeros_like(corner)

    def project(block):
        w_one = wp[...].astype(F32)
        w_rows = jnp.concatenate([w_one, w_one], axis=0)
        first_half = lax.broadcasted_iota(jnp.int32, w_rows.shape, 0) < heads
        w_both = jnp.concatenate(
            [jnp.where(first_half, w_rows, 0.0), jnp.where(first_half, 0.0, w_rows)], axis=1
        ).astype(BF16)
        count = half_t * block.shape[1]
        low = block[:half_t].reshape(count, chan)
        high = block[half_t:].reshape(count, chan)
        return dot_nt(w_both, jnp.concatenate([low, high], axis=1))

    def corner_send_copy():
        return pltpu.make_async_remote_copy(
            src_ref=csend,
            dst_ref=corner,
            send_sem=corner_send,
            recv_sem=corner_recv,
            device_id=(row, corner_to),
            device_id_type=MESH,
        )

    def table_send_copy(s):
        j = (col + 1 + s) % n_col
        return pltpu.make_async_remote_copy(
            src_ref=tsend.at[s],
            dst_ref=table,
            send_sem=table_send,
            recv_sem=table_recv,
            device_id=(row, j),
            device_id_type=MESH,
        )

    toks_copy.wait()
    mask_copy.wait()
    spare = 2 * width - atoms
    tokens = jnp.concatenate(
        [tok[...].reshape(1, atoms), jnp.full((1, spare), -1, jnp.int32)], axis=1
    )
    masks = jnp.concatenate(
        [mask[...].reshape(1, atoms), jnp.zeros((1, spare), jnp.int32)], axis=1
    )
    codes = jnp.where(masks == 1, tokens, -1)
    codes0, codes1 = codes[:, :width], codes[:, width:]
    messages[0] = jnp.broadcast_to(pltpu.roll(codes0, margin, 1), (8, width))
    messages[1] = jnp.broadcast_to(pltpu.roll(codes1, margin, 1), (8, width))

    def halo(i, src, dst, device):
        return pltpu.make_async_remote_copy(
            src_ref=src,
            dst_ref=dst,
            send_sem=halo_send.at[i],
            recv_sem=halo_recv.at[i],
            device_id=device,
            device_id_type=MESH,
        )

    x_left, x_right = pl.ds(atoms, margin), pl.ds(2 * width + margin, margin)
    to_left = (
        halo(0, xs.at[pl.ds(0, margin)], xs.at[x_right], left_id),
        halo(1, messages.at[0], codes_s.at[2], left_id),
    )
    to_right = (
        halo(2, xs.at[pl.ds(tail, margin)], xs.at[x_left], right_id),
        halo(3, messages.at[1], codes_s.at[1], right_id),
    )

    @pl.when(jnp.logical_not(has_left))
    def _():
        xs[x_left] = jnp.zeros((margin, width), BF16)
        codes_s[1] = jnp.full((8, width), -1, jnp.int32)

    @pl.when(jnp.logical_not(has_right))
    def _():
        xs[x_right] = jnp.zeros((margin, width), BF16)
        codes_s[2] = jnp.full((8, width), -1, jnp.int32)

    wp_copy.wait()
    group = n_col // 2

    @pl.when(is_holder)
    def _():
        for first in range(0, n_col, group):
            for s in range(first, first + group):
                strip_copy(s).wait()
            for s in range(first, first + group):
                tsend[s] = project(strips[s])

    x_copy.wait()
    pl.semaphore_wait(barrier, expected)

    @pl.when(is_holder)
    def _():
        for s in range(n_col - 1):
            table_send_copy(s).start()
        table[...] = tsend[n_col - 1]

    @pl.when(has_left)
    def _():
        for copy in to_left:
            copy.start()

    @pl.when(has_right)
    def _():
        for copy in to_right:
            copy.start()

    @pl.when(gives_corner)
    def _():
        corner_copy.wait()
        csend[...] = project(corner_x[...])

    @pl.when(corner_away)
    def _():
        corner_send_copy().start()

    @pl.when(gives_corner & takes_corner)
    def _():
        corner[...] = csend[...]

    used = 2 * heads * half_t
    wq_copy.wait()
    wg_copy.wait()
    wkv_copy.wait()
    shift_copy.wait()
    x_own = xs[pl.ds(0, atoms)]
    queries = dot(x_own, wq[...])
    gates = jax.nn.sigmoid(dot(x_own, wg[...]))
    lanes = lax.broadcasted_iota(jnp.int32, (atoms, width), 1)
    local_tok = tokens - tok_dev * me
    upper = local_tok >= half_t
    place = jnp.where(upper, (local_tok - half_t) * 8 + heads, local_tok * 8)
    place = jnp.transpose(jnp.broadcast_to(place, (width, 2 * width)))[:atoms]
    mark = used + lax.broadcasted_iota(jnp.int32, (atoms, width), 0) // QB
    for h in range(heads):
        q_h = jnp.where(lanes // head_dim == h, queries, 0.0).astype(BF16)
        hot_h = ((lanes == place + h) | (lanes == mark)).astype(F32).astype(BF16)
        low, high = pl.ds(h * tail, tail), pl.ds(heads * tail + h * margin, margin)
        lhs[low, pl.ds(0, width)] = q_h[:tail]
        lhs[low, pl.ds(width, width)] = hot_h[:tail]
        lhs[high, pl.ds(0, width)] = q_h[tail:]
        lhs[high, pl.ds(width, width)] = hot_h[tail:]
    member = lax.broadcasted_iota(jnp.int32, (32, atoms), 0) == (codes - tok_dev * me)[:, :atoms]
    member = member.astype(F32)
    count = jnp.sum(member, axis=1, keepdims=True)
    inverse = 1.0 / jnp.maximum(count, 1.0)
    member = member.astype(BF16)

    head_of = lax.broadcasted_iota(jnp.int32, (width, width), 1) // head_dim

    def place_keyval(b, keyval):
        rhs[b, pl.ds(0, width), :] = jnp.transpose(keyval[:, :width]).astype(BF16)
        for h in range(heads):
            vals[b, h, :, pl.ds(0, width)] = jnp.where(
                head_of == h, keyval[:, width:], 0.0
            ).astype(BF16)

    for h in range(heads):
        mine = (head_of == h).astype(F32).astype(BF16)
        for b in range(3):
            vals[b, h, :, pl.ds(width, width)] = mine

    place_keyval(0, dot(xs[pl.ds(0, width)], wkv[...]))
    side = lax.broadcasted_iota(jnp.int32, (1, width), 1)
    rest_rows = width - used
    sub = lax.broadcasted_iota(jnp.int32, (rest_rows, width), 0)
    starts = jnp.zeros((rest_rows, width), jnp.int32)
    n_blocks = atoms // QB
    for b in range(n_blocks):
        starts = jnp.where(sub == b, QB * b - KW // 2 + QB // 2 + shift[b], starts)

    def place_mask(b, at, code):
        inside = (at >= starts) & (at < starts + KW)
        value = jnp.where(inside, jnp.where(code >= 0, 0.0, DEAD), OUTSIDE)
        rhs[b, pl.ds(width + used, rest_rows), :] = jnp.where(sub < n_blocks, value, 0.0).astype(
            BF16
        )
        for k in (2, 3):
            rhs[b, pl.ds(k * width + used, rest_rows), :] = jnp.zeros((rest_rows, width), BF16)

    place_mask(0, side, codes0)
    tail_copy.wait()

    @pl.when(has_left)
    def _():
        for copy in to_right:
            copy.wait_recv()

    @pl.when(has_right)
    def _():
        for copy in to_left:
            copy.wait_recv()

    keyval = dot(xs[pl.ds(width, 2 * width)], wkv[...])
    place_keyval(1, keyval[:width])
    place_keyval(2, keyval[width:])
    codes_a = jnp.where(side < margin, codes1, codes_s[1][0:1])
    codes_b = jnp.where(side < margin, codes1, codes_s[2][0:1])
    place_mask(1, jnp.where(side < margin, side + width, side - width), codes_a)
    place_mask(2, side + width, codes_b)

    @pl.when(jnp.logical_not(is_holder))
    def _():
        table_send_copy(0).wait_recv()

    @pl.when(corner_comes)
    def _():
        corner_send_copy().wait_recv()

    main = table[...] * math.sqrt(head_dim)
    edge = corner[...] * math.sqrt(head_dim)
    stacked = jnp.concatenate(
        [
            jnp.concatenate(
                [main[:, WIDE * t : WIDE * (t + 1)], edge[:, SIDE * t : SIDE * (t + 1)]], axis=1
            )
            for t in range(half_t)
        ],
        axis=0,
    )
    first_token = hold_col * tok_cols + strip_start(col)

    def place_bias(b, code):
        index = jnp.broadcast_to((code - first_token) & (width - 1), (used, width))
        whole = jnp.take_along_axis(stacked, index, axis=1, mode="promise_in_bounds")
        high = whole.astype(BF16)
        rest = whole - high.astype(F32)
        mid = rest.astype(BF16)
        rhs[b, pl.ds(width, used), :] = high
        rhs[b, pl.ds(2 * width, used), :] = mid
        rhs[b, pl.ds(3 * width, used), :] = (rest - mid.astype(F32)).astype(BF16)

    place_bias(0, codes0)
    place_bias(1, codes_a)
    place_bias(2, codes_b)
    log_scale = math.log2(math.e) / math.sqrt(head_dim)

    def attend(first_row, n_rows, which):
        both = lhs[pl.ds(first_row, heads * n_rows), :]
        hot = both[:, width:]
        left = jnp.concatenate([both, hot, hot], axis=1)
        scores = dot(left, jnp.concatenate([rhs[0], rhs[which]], axis=1))
        parts = []
        for h in range(heads):
            part = scores[h * n_rows : (h + 1) * n_rows]
            top = jnp.max(part, axis=1, keepdims=True)
            parts.append(jnp.exp2((part - top) * log_scale).astype(BF16))
        by_head = [vals[b, h] for h in range(heads) for b in (0, which)]
        mixed = dot(jnp.concatenate(parts, axis=1), jnp.concatenate(by_head, axis=0))
        return mixed[:, :width] / mixed[:, width:]

    out_a = attend(0, tail, 1)
    out_b = attend(heads * tail, margin, 2)
    attended = (gates * jnp.concatenate([out_a, out_b], axis=0)).astype(BF16)
    wo_copy.wait()
    new_atoms = (x_own.astype(F32) + dot(attended, wo[...])).astype(BF16)
    atoms_out[...] = new_atoms
    wa_copy.wait()
    share = wa_in.shape[1] // n_col
    lifted = jnp.maximum(dot(new_atoms, wa[...]), 0.0).astype(BF16)
    means = (dot(member, lifted) * inverse)[:tok_dev]
    for c in range(n_col):
        if c * share + width <= means.shape[1]:
            piece = means[:, c * share : c * share + width]
        else:
            piece = pltpu.roll(means[:, -width:], share, 1)
        tok_send[c] = piece.astype(BF16)

    def tok_copy(other):
        return pltpu.make_async_remote_copy(
            src_ref=tok_send.at[other],
            dst_ref=tok_recv.at[col],
            send_sem=tok_ssem,
            recv_sem=tok_rsem,
            device_id=(row, other),
            device_id_type=MESH,
        )

    for step in range(1, n_col):
        tok_copy((col + step) % n_col).start()
    tok_recv[col] = tok_send[col]
    others = pl.ds(0, n_col - 1)
    all_tokens = pltpu.make_async_remote_copy(
        src_ref=tok_send.at[others],
        dst_ref=tok_recv.at[others],
        send_sem=tok_ssem,
        recv_sem=tok_rsem,
        device_id=(row, (col + 1) % n_col),
        device_id_type=MESH,
    )
    all_tokens.wait_recv()

    all_tokens.wait_send()

    @pl.when(is_holder)
    def _():
        pltpu.make_async_remote_copy(
            src_ref=tsend.at[others],
            dst_ref=tsend.at[others],
            send_sem=table_send,
            recv_sem=table_recv,
            device_id=(row, (col + 1) % n_col),
            device_id_type=MESH,
        ).wait_send()

    @pl.when(corner_away)
    def _():
        corner_send_copy().wait_send()

    @pl.when(has_left)
    def _():
        for copy in to_left:
            copy.wait_send()

    @pl.when(has_right)
    def _():
        for copy in to_right:
            copy.wait_send()


def finish(atoms_ref, gathered, atoms_out, token_out, token_v, sems):
    atoms_copy = pltpu.make_async_copy(atoms_ref, atoms_out, sems.at[0])
    atoms_copy.start()
    rows = jnp.concatenate(
        [gathered[c].astype(F32) for c in range(gathered.shape[0])], axis=0
    )
    token_v[...] = rows.astype(BF16)[:, : token_v.shape[1]]
    token_copy = pltpu.make_async_copy(token_v, token_out, sems.at[1])
    token_copy.start()
    atoms_copy.wait()
    token_copy.wait()


def per_device(n_row, n_col, *args):
    x, pair, w_pair, w_query, w_keyval, w_gate, w_out, w_agg, tok, shift, mask = args
    w_pair = w_pair.T
    atoms, width = x.shape
    tok_rows, tok_cols, chan = pair.shape
    heads = w_pair.shape[0]
    tok_dev = tok_rows // n_col
    half_t = tok_dev // 2
    ct = w_agg.shape[1]
    margin = KW // 2
    hbm = pl.BlockSpec(memory_space=pltpu.HBM)
    vmem = pl.BlockSpec(memory_space=pltpu.VMEM)
    dma = pltpu.SemaphoreType.DMA
    scratch = [
        pltpu.VMEM((3 * width, width), BF16),
        pltpu.VMEM((n_col, tok_dev, WIDE, chan), BF16),
        pltpu.VMEM((tok_dev, SIDE, chan), BF16),
        pltpu.VMEM(w_pair.shape, BF16),
        pltpu.VMEM(w_query.shape, BF16),
        pltpu.VMEM(w_keyval.shape, BF16),
        pltpu.VMEM(w_gate.shape, BF16),
        pltpu.VMEM(w_out.shape, BF16),
        pltpu.VMEM(w_agg.shape, BF16),
        pltpu.VMEM(tok.shape, jnp.int32),
        pltpu.VMEM(mask.shape, jnp.int32),
        pltpu.SMEM(shift.shape, jnp.int32),
        pltpu.VMEM((n_col, 2 * heads, half_t * WIDE), F32),
        pltpu.VMEM((2 * heads, half_t * SIDE), F32),
        pltpu.VMEM((2 * heads, half_t * WIDE), F32),
        pltpu.VMEM((2 * heads, half_t * SIDE), F32),
        pltpu.VMEM((2, 8, width), jnp.int32),
        pltpu.VMEM((3, 8, width), jnp.int32),
        pltpu.VMEM((heads * atoms, 2 * width), BF16),
        pltpu.VMEM((3, 4 * width, width), BF16),
        pltpu.VMEM((3, heads, width, 2 * width), BF16),
        pltpu.VMEM((n_col, tok_dev, width), BF16),
        dma((12,)),
        dma((n_col,)),
        dma((4,)),
        dma((4,)),
        dma,
        dma,
        dma,
        dma,
        dma,
        dma,
    ]
    inputs = (x, pair, w_pair, w_query, w_keyval, w_gate, w_out, w_agg, tok, shift, mask)
    inputs = [pltpu.with_memory_space_constraint(a, pltpu.HBM) for a in inputs]
    new_atoms, gathered = pl.pallas_call(
        functools.partial(kernel, n_row, n_col),
        out_shape=(
            pltpu.VMEM((atoms, width), BF16),
            pltpu.VMEM((n_col, tok_dev, width), BF16),
        ),
        in_specs=[hbm] * 11,
        out_specs=(vmem, vmem),
        scratch_shapes=scratch,
        compiler_params=pltpu.CompilerParams(
            collective_id=0, has_side_effects=True, vmem_limit_bytes=40 * 1024 * 1024
        ),
        name="atom_block",
    )(*inputs)
    return pl.pallas_call(
        finish,
        out_shape=(
            pltpu.HBM((atoms, width), BF16),
            pltpu.HBM((tok_rows, ct // n_col), BF16),
        ),
        in_specs=[vmem, vmem],
        out_specs=(hbm, hbm),
        scratch_shapes=[pltpu.VMEM((tok_rows, ct // n_col), BF16), dma((2,))],
        compiler_params=pltpu.CompilerParams(vmem_limit_bytes=8 * 1024 * 1024),
        name="write_out",
    )(new_atoms, gathered)


def solution(mesh):
    n_row, n_col = mesh.shape["row"], mesh.shape["col"]
    split = P(("row", "col"))
    in_specs = (
        P(("row", "col"), None),
        P("row", "col", None),
        P(),
        P(),
        P(),
        P(),
        P(),
        P(),
        split,
        split,
        split,
    )
    out_specs = (P(("row", "col"), None), P("row", "col"))
    return jax.shard_map(
        functools.partial(per_device, n_row, n_col),
        mesh=mesh,
        in_specs=in_specs,
        out_specs=out_specs,
        check_vma=False,
    )
```

time: 20.9 us -> 20.8 us (level)
  the two profiles are of different devices: /device:TPU:1 before, /device:TPU:0 now
where the time goes in v2:
time: 20.8 us; the launch traced here: 20.7 us
  Pallas kernels  20.1 us (97%)
  between operations  0.64 us (3%)
    pallas_call x1, Pallas kernels, per_device(): pl.pallas_call(functools.partial(kernel, n_row, n_col), out_shape=(pltpu....  19.4 us
    pallas_call x1, Pallas kernels, per_device(): pl.pallas_call(finish, out_shape=(pltpu.HBM((atoms, width), BF16), pltpu....  0.66 us

profile of v2, /device:TPU:0, one launch (start us, length us, event | category | flops | bytes accessed | tf_op | source)
XLA Modules:
  0.0 20.7 jit_solution(10862245011288114734)
XLA Ops:
  0.6 19.4 %atom_block.1 = (bf16[192,128]{1,0:T(8,128)(2,1)S(1)}, bf16[8,24,128]{2,1,0:T(8,128)(2,1)S(1)}) custom-call(bf16[192,128]{1,0:T(8,128)(2,1)} %x_in.1, bf16[192,384,128]{2,1,0:T(8,128)(2,1)} %pair_in.1, bf16[4,128]{1,0:T(4,128)(2,1)} %bitcast.1, bf16[128,128]{1,0:T(8,128)(2,1)} %wq_in.1, bf16[128,256]{1,0:T(8,128)(2,1)} %wkv_in.1, bf16[128,128]{1,0:T(8,128)(2,1)} %wg_in.1, ...), custom_call_target="tpu_custom_call" | custom-call | tf_op jit(solution)/shard_map/atom_block/pallas_call | solution.py:569
  20.1 0.7 %write_out.1 = (bf16[192,128]{1,0:T(8,128)(2,1)}, bf16[192,96]{1,0:T(8,128)(2,1)}) custom-call(bf16[192,128]{1,0:T(8,128)(2,1)S(1)} %get-tuple-element.4.atoms_ref, bf16[8,24,128]{2,1,0:T(8,128)(2,1)S(1)} %get-tuple-element.5.gathered), custom_call_target="tpu_custom_call" | custom-call | tf_op jit(solution)/shard_map/write_out/pallas_call | solution.py:583

commit v3 on v2

--- a/solution.py
+++ b/solution.py
@@ -12,8 +12,7 @@
 
 QB = 32
 KW = 128
-WIDE = 80
-SIDE = 48
+WIDE = 72
 OUTSIDE = -(2.0**126)
 DEAD = -(2.0**100)
 F32 = jnp.float32
@@ -53,6 +52,7 @@
     wg,
     wo,
     wa,
+    wa_pad,
     tok,
     mask,
     shift,
@@ -68,6 +68,7 @@
     tok_send,
     in_sem,
     strip_sem,
+    corner_sem,
     halo_send,
     halo_recv,
     table_send,
@@ -97,9 +98,15 @@
     has_left = me > 0
     has_right = me < n_dev - 1
 
+    def nth(s):
+        half = n_col // 2
+        turn = (half // 2, 1, half - 1, 0)[s % half]
+        side = col // half if s >= half else 1 - col // half
+        return side * half + (col + turn) % half
+
     def strip_start(j):
         want = jnp.maximum(base + tok_dev * (j - 1), 0)
-        return jnp.minimum((want // 16) * 16, tok_cols - WIDE)
+        return jnp.minimum(want, tok_cols - WIDE)
 
     barrier = pltpu.get_barrier_semaphore()
 
@@ -138,14 +145,20 @@
     wo_copy = local(9, wo_in, wo)
     wa_copy = local(10, wa_in, wa)
 
-    def strip_copy(s):
-        j = (col + 1 + s) % n_col
-        start = pl.multiple_of(strip_start(j), 16)
-        return pltpu.make_async_copy(
-            pair_in.at[pl.ds(pl.multiple_of(tok_dev * j, 8), tok_dev), pl.ds(start, WIDE)],
-            strips.at[s],
-            strip_sem.at[s],
-        )
+    def window_copies(first_row, first_col, dst, sems):
+        return [
+            pltpu.make_async_copy(
+                pair_in.at[pl.ds(first_row + p * half_t, half_t), pl.ds(first_col, WIDE)],
+                dst.at[:, pl.ds(p * WIDE, WIDE)],
+                sems.at[p],
+            )
+            for p in range(2)
+        ]
+
+    def strip_copies(s):
+        j = nth(s)
+        start = pl.multiple_of(strip_start(j), 8)
+        return window_copies(tok_dev * j, start, strips.at[s], strip_sem.at[s])
 
     x_copy.start()
     toks_copy.start()
@@ -155,7 +168,8 @@
     @pl.when(is_holder)
     def _():
         for s in range(n_col):
-            strip_copy(s).start()
+            for copy in strip_copies(s):
+                copy.start()
 
     wq_copy.start()
     wg_copy.start()
@@ -170,15 +184,14 @@
     takes_corner = (up_row & even) | (down_row & odd)
     corner_comes = takes_corner & jnp.logical_not(gives_corner)
     corner_away = gives_corner & jnp.logical_not(takes_corner)
-    corner_col = pl.multiple_of(jnp.where(even, tok_cols - SIDE, 0), 16)
+    corner_col = pl.multiple_of(jnp.where(even, tok_cols - WIDE, 0), 8)
     corner_row = pl.multiple_of(jnp.where(even, 0, tok_rows - tok_dev), 8)
-    corner_copy = pltpu.make_async_copy(
-        pair_in.at[pl.ds(corner_row, tok_dev), pl.ds(corner_col, SIDE)], corner_x, in_sem.at[11]
-    )
+    corner_copies = window_copies(corner_row, corner_col, corner_x, corner_sem)
 
     @pl.when(gives_corner)
     def _():
-        corner_copy.start()
+        for copy in corner_copies:
+            copy.start()
 
     @pl.when(jnp.logical_not(corner_comes))
     def _():
@@ -191,10 +204,11 @@
         w_both = jnp.concatenate(
             [jnp.where(first_half, w_rows, 0.0), jnp.where(first_half, 0.0, w_rows)], axis=1
         ).astype(BF16)
-        count = half_t * block.shape[1]
-        low = block[:half_t].reshape(count, chan)
-        high = block[half_t:].reshape(count, chan)
-        return dot_nt(w_both, jnp.concatenate([low, high], axis=1))
+        flat = block.reshape(tok_dev * WIDE, chan)
+        low, high = flat[: half_t * WIDE], flat[half_t * WIDE :]
+        out = dot_nt(w_both, jnp.concatenate([low, high], axis=1))
+        spare = table.shape[1] - out.shape[1]
+        return jnp.concatenate([out, jnp.zeros((2 * heads, spare), F32)], axis=1)
 
     def corner_send_copy():
         return pltpu.make_async_remote_copy(
@@ -207,7 +221,7 @@
         )
 
     def table_send_copy(s):
-        j = (col + 1 + s) % n_col
+        j = nth(s)
         return pltpu.make_async_remote_copy(
             src_ref=tsend.at[s],
             dst_ref=table,
@@ -261,39 +275,29 @@
         xs[x_right] = jnp.zeros((margin, width), BF16)
         codes_s[2] = jnp.full((8, width), -1, jnp.int32)
 
-    wp_copy.wait()
-    group = n_col // 2
-
-    @pl.when(is_holder)
-    def _():
-        for first in range(0, n_col, group):
-            for s in range(first, first + group):
-                strip_copy(s).wait()
-            for s in range(first, first + group):
-                tsend[s] = project(strips[s])
-
     x_copy.wait()
-    pl.semaphore_wait(barrier, expected)
-
-    @pl.when(is_holder)
-    def _():
-        for s in range(n_col - 1):
-            table_send_copy(s).start()
-        table[...] = tsend[n_col - 1]
-
-    @pl.when(has_left)
-    def _():
-        for copy in to_left:
-            copy.start()
-
-    @pl.when(has_right)
-    def _():
-        for copy in to_right:
-            copy.start()
+
+    def send_halos():
+        @pl.when(has_left)
+        def _():
+            for copy in to_left:
+                copy.start()
+
+        @pl.when(has_right)
+        def _():
+            for copy in to_right:
+                copy.start()
+
+    @pl.when(jnp.logical_not(is_holder))
+    def _():
+        pl.semaphore_wait(barrier, expected)
+        send_halos()
 
     @pl.when(gives_corner)
     def _():
-        corner_copy.wait()
+        wp_copy.wait()
+        for copy in corner_copies:
+            copy.wait()
         csend[...] = project(corner_x[...])
 
     @pl.when(corner_away)
@@ -314,8 +318,10 @@
     gates = jax.nn.sigmoid(dot(x_own, wg[...]))
     lanes = lax.broadcasted_iota(jnp.int32, (atoms, width), 1)
     local_tok = tokens - tok_dev * me
-    upper = local_tok >= half_t
-    place = jnp.where(upper, (local_tok - half_t) * 8 + heads, local_tok * 8)
+    second = (local_tok >= half_t).astype(jnp.int32)
+    within = local_tok - half_t * second
+    lower = (within >= half_t // 2).astype(jnp.int32)
+    place = 2 * heads * (2 * within - half_t * lower + second) + heads * lower
     place = jnp.transpose(jnp.broadcast_to(place, (width, 2 * width)))[:atoms]
     mark = used + lax.broadcasted_iota(jnp.int32, (atoms, width), 0) // QB
     for h in range(heads):
@@ -326,11 +332,38 @@
         lhs[low, pl.ds(width, width)] = hot_h[:tail]
         lhs[high, pl.ds(0, width)] = q_h[tail:]
         lhs[high, pl.ds(width, width)] = hot_h[tail:]
+    wa_copy.wait()
+    share = wa_in.shape[1] // n_col
+    for c in range(n_col):
+        wa_pad[:, c * width : (c + 1) * width] = jnp.concatenate(
+            [wa[:, c * share : (c + 1) * share], jnp.zeros((width, width - share), BF16)], axis=1
+        )
     member = lax.broadcasted_iota(jnp.int32, (32, atoms), 0) == (codes - tok_dev * me)[:, :atoms]
     member = member.astype(F32)
     count = jnp.sum(member, axis=1, keepdims=True)
     inverse = 1.0 / jnp.maximum(count, 1.0)
     member = member.astype(BF16)
+
+    @pl.when(is_holder)
+    def _():
+        wp_copy.wait()
+        group = n_col // 2
+        for begin in range(0, n_col, group):
+            for s in range(begin, begin + group):
+                for copy in strip_copies(s):
+                    copy.wait()
+            for s in range(begin, begin + group):
+                tsend[s] = project(strips[s])
+            if begin == 0:
+                pl.semaphore_wait(barrier, expected)
+                send_halos()
+            for s in range(begin, min(begin + group, n_col - 1)):
+                table_send_copy(s).start()
+        table[...] = tsend[n_col - 1]
+
+    @pl.when(jnp.logical_not(is_holder | gives_corner))
+    def _():
+        wp_copy.wait()
 
     head_of = lax.broadcasted_iota(jnp.int32, (width, width), 1) // head_dim
 
@@ -385,6 +418,12 @@
     place_mask(1, jnp.where(side < margin, side + width, side - width), codes_a)
     place_mask(2, side + width, codes_b)
 
+    first_token = hold_col * tok_cols + strip_start(col)
+    in_strip = lax.broadcasted_iota(jnp.int32, table.shape, 1) % WIDE
+    from_low = in_strip >= jnp.where(takes_corner & even, WIDE - tok_dev, WIDE)
+    from_high = in_strip < jnp.where(takes_corner & odd, tok_dev, 0)
+    from_corner = from_low | from_high
+
     @pl.when(jnp.logical_not(is_holder))
     def _():
         table_send_copy(0).wait_recv()
@@ -393,22 +432,26 @@
     def _():
         corner_send_copy().wait_recv()
 
-    main = table[...] * math.sqrt(head_dim)
-    edge = corner[...] * math.sqrt(head_dim)
-    stacked = jnp.concatenate(
-        [
-            jnp.concatenate(
-                [main[:, WIDE * t : WIDE * (t + 1)], edge[:, SIDE * t : SIDE * (t + 1)]], axis=1
-            )
-            for t in range(half_t)
-        ],
-        axis=0,
-    )
-    first_token = hold_col * tok_cols + strip_start(col)
+    main = jnp.where(from_corner, corner[...], table[...]) * math.sqrt(head_dim)
 
     def place_bias(b, code):
-        index = jnp.broadcast_to((code - first_token) & (width - 1), (used, width))
-        whole = jnp.take_along_axis(stacked, index, axis=1, mode="promise_in_bounds")
+        index = code - first_token
+        index = jnp.where(index < 0, index + WIDE, jnp.where(index >= WIDE, index - WIDE, index))
+        index = jnp.broadcast_to(jnp.clip(index, 0, WIDE - 1), (2 * heads, width))
+        rows = []
+        for t in range(half_t):
+            a, at = divmod(WIDE * t, width)
+            flat = index + at
+
+            def take(k):
+                tile = main[:, k * width : (k + 1) * width]
+                return jnp.take_along_axis(
+                    tile, flat & (width - 1), axis=1, mode="promise_in_bounds"
+                )
+
+            one = take(a)
+            rows.append(one if at + WIDE <= width else jnp.where(flat < width, one, take(a + 1)))
+        whole = jnp.concatenate(rows, axis=0)
         high = whole.astype(BF16)
         rest = whole - high.astype(F32)
         mid = rest.astype(BF16)
@@ -441,16 +484,10 @@
     wo_copy.wait()
     new_atoms = (x_own.astype(F32) + dot(attended, wo[...])).astype(BF16)
     atoms_out[...] = new_atoms
-    wa_copy.wait()
-    share = wa_in.shape[1] // n_col
-    lifted = jnp.maximum(dot(new_atoms, wa[...]), 0.0).astype(BF16)
-    means = (dot(member, lifted) * inverse)[:tok_dev]
+    lifted = jnp.maximum(dot(new_atoms, wa_pad[...]), 0.0).astype(BF16)
+    means = (dot(member, lifted) * inverse)[:tok_dev].astype(BF16)
     for c in range(n_col):
-        if c * share + width <= means.shape[1]:
-            piece = means[:, c * share : c * share + width]
-        else:
-            piece = pltpu.roll(means[:, -width:], share, 1)
-        tok_send[c] = piece.astype(BF16)
+        tok_send[c] = means[:, c * width : (c + 1) * width]
 
     def tok_copy(other):
         return pltpu.make_async_remote_copy(
@@ -462,8 +499,8 @@
             device_id_type=MESH,
         )
 
-    for step in range(1, n_col):
-        tok_copy((col + step) % n_col).start()
+    for s in range(n_col - 1):
+        tok_copy(nth(s)).start()
     tok_recv[col] = tok_send[col]
     others = pl.ds(0, n_col - 1)
     all_tokens = pltpu.make_async_remote_copy(
@@ -527,34 +564,37 @@
     half_t = tok_dev // 2
     ct = w_agg.shape[1]
     margin = KW // 2
+    lanes = -(-half_t * WIDE // 128) * 128
     hbm = pl.BlockSpec(memory_space=pltpu.HBM)
     vmem = pl.BlockSpec(memory_space=pltpu.VMEM)
     dma = pltpu.SemaphoreType.DMA
     scratch = [
         pltpu.VMEM((3 * width, width), BF16),
-        pltpu.VMEM((n_col, tok_dev, WIDE, chan), BF16),
-        pltpu.VMEM((tok_dev, SIDE, chan), BF16),
+        pltpu.VMEM((n_col, half_t, 2 * WIDE, chan), BF16),
+        pltpu.VMEM((half_t, 2 * WIDE, chan), BF16),
         pltpu.VMEM(w_pair.shape, BF16),
         pltpu.VMEM(w_query.shape, BF16),
         pltpu.VMEM(w_keyval.shape, BF16),
         pltpu.VMEM(w_gate.shape, BF16),
         pltpu.VMEM(w_out.shape, BF16),
         pltpu.VMEM(w_agg.shape, BF16),
+        pltpu.VMEM((width, n_col * width), BF16),
         pltpu.VMEM(tok.shape, jnp.int32),
         pltpu.VMEM(mask.shape, jnp.int32),
         pltpu.SMEM(shift.shape, jnp.int32),
-        pltpu.VMEM((n_col, 2 * heads, half_t * WIDE), F32),
-        pltpu.VMEM((2 * heads, half_t * SIDE), F32),
-        pltpu.VMEM((2 * heads, half_t * WIDE), F32),
-        pltpu.VMEM((2 * heads, half_t * SIDE), F32),
+        pltpu.VMEM((n_col, 2 * heads, lanes), F32),
+        pltpu.VMEM((2 * heads, lanes), F32),
+        pltpu.VMEM((2 * heads, lanes), F32),
+        pltpu.VMEM((2 * heads, lanes), F32),
         pltpu.VMEM((2, 8, width), jnp.int32),
         pltpu.VMEM((3, 8, width), jnp.int32),
         pltpu.VMEM((heads * atoms, 2 * width), BF16),
         pltpu.VMEM((3, 4 * width, width), BF16),
         pltpu.VMEM((3, heads, width, 2 * width), BF16),
         pltpu.VMEM((n_col, tok_dev, width), BF16),
-        dma((12,)),
-        dma((n_col,)),
+        dma((11,)),
+        dma((n_col, 2)),
+        dma((2,)),
         dma((4,)),
         dma((4,)),
         dma,

time: 20.8 us -> 20.3 us (0.976)
  the two profiles are of different devices: /device:TPU:0 before, /device:TPU:1 now
where the time goes in v3:
time: 20.3 us; the launch traced here: 20.1 us
  Pallas kernels  19.5 us (96%)
  between operations  0.64 us (3%)
    pallas_call x1, Pallas kernels, per_device(): pl.pallas_call(functools.partial(kernel, n_row, n_col), out_shape=(pltpu....  18.8 us
    pallas_call x1, Pallas kernels, per_device(): pl.pallas_call(finish, out_shape=(pltpu.HBM((atoms, width), BF16), pltpu....  0.66 us

profile of v3, /device:TPU:1, one launch (start us, length us, event | category | flops | bytes accessed | tf_op | source)
XLA Modules:
  0.0 20.1 jit_solution(9847288384747226970)
XLA Ops:
  0.6 18.8 %atom_block.1 = (bf16[192,128]{1,0:T(8,128)(2,1)S(1)}, bf16[8,24,128]{2,1,0:T(8,128)(2,1)S(1)}) custom-call(bf16[192,128]{1,0:T(8,128)(2,1)} %x_in.1, bf16[192,384,128]{2,1,0:T(8,128)(2,1)} %pair_in.1, bf16[4,128]{1,0:T(4,128)(2,1)} %bitcast.1, bf16[128,128]{1,0:T(8,128)(2,1)} %wq_in.1, bf16[128,256]{1,0:T(8,128)(2,1)} %wkv_in.1, bf16[128,128]{1,0:T(8,128)(2,1)} %wg_in.1, ...), custom_call_target="tpu_custom_call" | custom-call | tf_op jit(solution)/shard_map/atom_block/pallas_call | solution.py:609
  19.5 0.7 %write_out.1 = (bf16[192,128]{1,0:T(8,128)(2,1)}, bf16[192,96]{1,0:T(8,128)(2,1)}) custom-call(bf16[192,128]{1,0:T(8,128)(2,1)S(1)} %get-tuple-element.4.atoms_ref, bf16[8,24,128]{2,1,0:T(8,128)(2,1)S(1)} %get-tuple-element.5.gathered), custom_call_target="tpu_custom_call" | custom-call | tf_op jit(solution)/shard_map/write_out/pallas_call | solution.py:623

commit v4 on v3

--- a/solution.py
+++ b/solution.py
@@ -344,27 +344,6 @@
     inverse = 1.0 / jnp.maximum(count, 1.0)
     member = member.astype(BF16)
 
-    @pl.when(is_holder)
-    def _():
-        wp_copy.wait()
-        group = n_col // 2
-        for begin in range(0, n_col, group):
-            for s in range(begin, begin + group):
-                for copy in strip_copies(s):
-                    copy.wait()
-            for s in range(begin, begin + group):
-                tsend[s] = project(strips[s])
-            if begin == 0:
-                pl.semaphore_wait(barrier, expected)
-                send_halos()
-            for s in range(begin, min(begin + group, n_col - 1)):
-                table_send_copy(s).start()
-        table[...] = tsend[n_col - 1]
-
-    @pl.when(jnp.logical_not(is_holder | gives_corner))
-    def _():
-        wp_copy.wait()
-
     head_of = lax.broadcasted_iota(jnp.int32, (width, width), 1) // head_dim
 
     def place_keyval(b, keyval):
@@ -398,6 +377,33 @@
             rhs[b, pl.ds(k * width + used, rest_rows), :] = jnp.zeros((rest_rows, width), BF16)
 
     place_mask(0, side, codes0)
+    group = n_col // 2
+    starts_early = hold_col % group < group // 2
+
+    def announce():
+        pl.semaphore_wait(barrier, expected)
+        send_halos()
+        for s in range(group):
+            table_send_copy(s).start()
+
+    @pl.when(is_holder)
+    def _():
+        wp_copy.wait()
+        for begin in range(0, n_col, group):
+            for s in range(begin, begin + group):
+                for copy in strip_copies(s):
+                    copy.wait()
+            for s in range(begin, begin + group):
+                tsend[s] = project(strips[s])
+            pl.when(starts_early == (begin > 0))(announce)
+        for s in range(group, n_col - 1):
+            table_send_copy(s).start()
+        table[...] = tsend[n_col - 1]
+
+    @pl.when(jnp.logical_not(is_holder | gives_corner))
+    def _():
+        wp_copy.wait()
+
     tail_copy.wait()
 
     @pl.when(has_left)
@@ -487,7 +493,7 @@
     lifted = jnp.maximum(dot(new_atoms, wa_pad[...]), 0.0).astype(BF16)
     means = (dot(member, lifted) * inverse)[:tok_dev].astype(BF16)
     for c in range(n_col):
-        tok_send[c] = means[:, c * width : (c + 1) * width]
+        tok_send[c] = means[:, c * width : c * width + share]
 
     def tok_copy(other):
         return pltpu.make_async_remote_copy(
@@ -547,7 +553,7 @@
     rows = jnp.concatenate(
         [gathered[c].astype(F32) for c in range(gathered.shape[0])], axis=0
     )
-    token_v[...] = rows.astype(BF16)[:, : token_v.shape[1]]
+    token_v[...] = rows.astype(BF16)
     token_copy = pltpu.make_async_copy(token_v, token_out, sems.at[1])
     token_copy.start()
     atoms_copy.wait()
@@ -591,7 +597,7 @@
         pltpu.VMEM((heads * atoms, 2 * width), BF16),
         pltpu.VMEM((3, 4 * width, width), BF16),
         pltpu.VMEM((3, heads, width, 2 * width), BF16),
-        pltpu.VMEM((n_col, tok_dev, width), BF16),
+        pltpu.VMEM((n_col, tok_dev, ct // n_col), BF16),
         dma((11,)),
         dma((n_col, 2)),
         dma((2,)),
@@ -610,7 +616,7 @@
         functools.partial(kernel, n_row, n_col),
         out_shape=(
             pltpu.VMEM((atoms, width), BF16),
-            pltpu.VMEM((n_col, tok_dev, width), BF16),
+            pltpu.VMEM((n_col, tok_dev, ct // n_col), BF16),
         ),
         in_specs=[hbm] * 11,
         out_specs=(vmem, vmem),

time: 20.3 us -> 20.2 us (level)
  no operation moved by 1% of the time
where the time goes in v4:
time: 20.2 us; the launch traced here: 20.1 us
  Pallas kernels  19.4 us (96%)
  between operations  0.64 us (3%)
    pallas_call x1, Pallas kernels, per_device(): pl.pallas_call(functools.partial(kernel, n_row, n_col), out_shape=(pltpu....  18.8 us
    pallas_call x1, Pallas kernels, per_device(): pl.pallas_call(finish, out_shape=(pltpu.HBM((atoms, width), BF16), pltpu....  0.66 us

profile of v4, /device:TPU:1, one launch (start us, length us, event | category | flops | bytes accessed | tf_op | source)
XLA Modules:
  0.0 20.1 jit_solution(7323417340746523110)
XLA Ops:
  0.6 18.8 %atom_block.1 = (bf16[192,128]{1,0:T(8,128)(2,1)S(1)}, bf16[8,24,96]{2,1,0:T(8,128)(2,1)S(1)}) custom-call(bf16[192,128]{1,0:T(8,128)(2,1)} %x_in.1, bf16[192,384,128]{2,1,0:T(8,128)(2,1)} %pair_in.1, bf16[4,128]{1,0:T(4,128)(2,1)} %bitcast.1, bf16[128,128]{1,0:T(8,128)(2,1)} %wq_in.1, bf16[128,256]{1,0:T(8,128)(2,1)} %wkv_in.1, bf16[128,128]{1,0:T(8,128)(2,1)} %wg_in.1, ...), custom_call_target="tpu_custom_call" | custom-call | tf_op jit(solution)/shard_map/atom_block/pallas_call | solution.py:615
  19.4 0.7 %write_out.1 = (bf16[192,128]{1,0:T(8,128)(2,1)}, bf16[192,96]{1,0:T(8,128)(2,1)}) custom-call(bf16[192,128]{1,0:T(8,128)(2,1)S(1)} %get-tuple-element.4.atoms_ref, bf16[8,24,96]{2,1,0:T(8,128)(2,1)S(1)} %get-tuple-element.5.gathered), custom_call_target="tpu_custom_call" | custom-call | tf_op jit(solution)/shard_map/write_out/pallas_call | solution.py:629

commit v5 on v4

--- a/solution.py
+++ b/solution.py
@@ -288,25 +288,12 @@
             for copy in to_right:
                 copy.start()
 
-    @pl.when(jnp.logical_not(is_holder))
+    comes_last = col == n_col - 1
+
+    @pl.when(jnp.logical_not(is_holder) & comes_last)
     def _():
         pl.semaphore_wait(barrier, expected)
         send_halos()
-
-    @pl.when(gives_corner)
-    def _():
-        wp_copy.wait()
-        for copy in corner_copies:
-            copy.wait()
-        csend[...] = project(corner_x[...])
-
-    @pl.when(corner_away)
-    def _():
-        corner_send_copy().start()
-
-    @pl.when(gives_corner & takes_corner)
-    def _():
-        corner[...] = csend[...]
 
     used = 2 * heads * half_t
     wq_copy.wait()
@@ -377,14 +364,34 @@
             rhs[b, pl.ds(k * width + used, rest_rows), :] = jnp.zeros((rest_rows, width), BF16)
 
     place_mask(0, side, codes0)
+    @pl.when(jnp.logical_not(is_holder | comes_last))
+    def _():
+        pl.semaphore_wait(barrier, expected)
+        send_halos()
+
+    @pl.when(gives_corner)
+    def _():
+        wp_copy.wait()
+        for copy in corner_copies:
+            copy.wait()
+        csend[...] = project(corner_x[...])
+
+    @pl.when(corner_away)
+    def _():
+        corner_send_copy().start()
+
+    @pl.when(gives_corner & takes_corner)
+    def _():
+        corner[...] = csend[...]
+
     group = n_col // 2
     starts_early = hold_col % group < group // 2
 
     def announce():
         pl.semaphore_wait(barrier, expected)
-        send_halos()
         for s in range(group):
             table_send_copy(s).start()
+        send_halos()
 
     @pl.when(is_holder)
     def _():

time: 20.2 us -> 20.1 us (level)
  no operation moved by 1% of the time
where the time goes in v5:
time: 20.1 us; the launch traced here: 20 us
  Pallas kernels  19.4 us (97%)
  between operations  0.64 us (3%)
    pallas_call x1, Pallas kernels, per_device(): pl.pallas_call(functools.partial(kernel, n_row, n_col), out_shape=(pltpu....  18.7 us
    pallas_call x1, Pallas kernels, per_device(): pl.pallas_call(finish, out_shape=(pltpu.HBM((atoms, width), BF16), pltpu....  0.66 us

profile of v5, /device:TPU:1, one launch (start us, length us, event | category | flops | bytes accessed | tf_op | source)
XLA Modules:
  0.0 20.0 jit_solution(9544236196630756862)
XLA Ops:
  0.6 18.7 %atom_block.1 = (bf16[192,128]{1,0:T(8,128)(2,1)S(1)}, bf16[8,24,96]{2,1,0:T(8,128)(2,1)S(1)}) custom-call(bf16[192,128]{1,0:T(8,128)(2,1)} %x_in.1, bf16[192,384,128]{2,1,0:T(8,128)(2,1)} %pair_in.1, bf16[4,128]{1,0:T(4,128)(2,1)} %bitcast.1, bf16[128,128]{1,0:T(8,128)(2,1)} %wq_in.1, bf16[128,256]{1,0:T(8,128)(2,1)} %wkv_in.1, bf16[128,128]{1,0:T(8,128)(2,1)} %wg_in.1, ...), custom_call_target="tpu_custom_call" | custom-call | tf_op jit(solution)/shard_map/atom_block/pallas_call | solution.py:622
  19.3 0.7 %write_out.1 = (bf16[192,128]{1,0:T(8,128)(2,1)}, bf16[192,96]{1,0:T(8,128)(2,1)}) custom-call(bf16[192,128]{1,0:T(8,128)(2,1)S(1)} %get-tuple-element.4.atoms_ref, bf16[8,24,96]{2,1,0:T(8,128)(2,1)S(1)} %get-tuple-element.5.gathered), custom_call_target="tpu_custom_call" | custom-call | tf_op jit(solution)/shard_map/write_out/pallas_call | solution.py:636

commit v6 on v5

--- a/solution.py
+++ b/solution.py
@@ -278,14 +278,14 @@
     x_copy.wait()
 
     def send_halos():
+        @pl.when(has_right)
+        def _():
+            for copy in to_right:
+                copy.start()
+
         @pl.when(has_left)
         def _():
             for copy in to_left:
-                copy.start()
-
-        @pl.when(has_right)
-        def _():
-            for copy in to_right:
                 copy.start()
 
     comes_last = col == n_col - 1

time: 20.1 us -> 20.1 us (level)
  no operation moved by 1% of the time
where the time goes in v6:
time: 20.1 us; the launch traced here: 20 us
  Pallas kernels  19.4 us (97%)
  between operations  0.64 us (3%)
    pallas_call x1, Pallas kernels, per_device(): pl.pallas_call(functools.partial(kernel, n_row, n_col), out_shape=(pltpu....  18.7 us
    pallas_call x1, Pallas kernels, per_device(): pl.pallas_call(finish, out_shape=(pltpu.HBM((atoms, width), BF16), pltpu....  0.66 us

profile of v6, /device:TPU:1, one launch (start us, length us, event | category | flops | bytes accessed | tf_op | source)
XLA Modules:
  0.0 20.0 jit_solution(5854188790245267643)
XLA Ops:
  0.6 18.7 %atom_block.1 = (bf16[192,128]{1,0:T(8,128)(2,1)S(1)}, bf16[8,24,96]{2,1,0:T(8,128)(2,1)S(1)}) custom-call(bf16[192,128]{1,0:T(8,128)(2,1)} %x_in.1, bf16[192,384,128]{2,1,0:T(8,128)(2,1)} %pair_in.1, bf16[4,128]{1,0:T(4,128)(2,1)} %bitcast.1, bf16[128,128]{1,0:T(8,128)(2,1)} %wq_in.1, bf16[128,256]{1,0:T(8,128)(2,1)} %wkv_in.1, bf16[128,128]{1,0:T(8,128)(2,1)} %wg_in.1, ...), custom_call_target="tpu_custom_call" | custom-call | tf_op jit(solution)/shard_map/atom_block/pallas_call | solution.py:622
  19.3 0.7 %write_out.1 = (bf16[192,128]{1,0:T(8,128)(2,1)}, bf16[192,96]{1,0:T(8,128)(2,1)}) custom-call(bf16[192,128]{1,0:T(8,128)(2,1)S(1)} %get-tuple-element.4.atoms_ref, bf16[8,24,96]{2,1,0:T(8,128)(2,1)S(1)} %get-tuple-element.5.gathered), custom_call_target="tpu_custom_call" | custom-call | tf_op jit(solution)/shard_map/write_out/pallas_call | solution.py:636
